TPU v7x, 512 devices: a whole 4x4x16 slice. The times are simulated.
512 devices in a mesh: boxes: 512 (over z, x, y, core).
Axes of the slice: x: 4, y: 4, z: 16, core: 2. Of those that a mesh axis runs over, the one named last changes fastest.
Arguments:
- coarse_state: float32 [512, 5, 512], P('boxes'), may hold values from -1 to 6, as said below
- fine_state: float32 [512, 8, 5, 512], P('boxes'), may hold values from -1 to 6, as said below
- refined: int32 [512, 8], P('boxes'), may hold values from 0 to 1, as said below
Outputs:
- coarse_out: float32 [512, 5, 512], P('boxes')
- fine_out: float32 [512, 8, 5, 512], P('boxes')
Inputs may be any that keep to these rules, and one draw needn't show every extreme that they name: `coarse_state`: per cell the five values are density, three momenta and total energy of a gas with density and pressure from 0.5 to 2 and each velocity component within 0.5. `fine_state`: per cell the five values are density, three momenta and total energy of a gas with density and pressure from 0.5 to 2 and each velocity component within 0.5. Each block has 1 to 4 refined octants, and some block has exactly 4.
All inputs are finite; a program needn't handle non-finite values.
Results may differ from a plain program's by a relative error of at most 0.0003.
Values sent between devices are 32-bit elements; how exact they have to be, the bound alone decides.
No kernel may reach another device: no remote copies, remote signals or barrier semaphores. Data moves between devices by JAX's collectives and lax.ppermute only.
A program may use at most 64 MiB of HBM per device.

v0:
```python
import functools

import jax
import jax.numpy as jnp
import ml_dtypes
import numpy as np
from jax import lax
from jax.experimental import pallas as pl
from jax.experimental.pallas import tpu as pltpu
from jax.sharding import PartitionSpec as P

PITCH = 10
LANES = 128
FINE = 40
COARSE = FINE
DEEP = COARSE + 5
COVER = DEEP + 5
COUNT = COVER + 1
ROWS0 = 56
INNER1 = 4 * 8
ROWS1 = INNER1 + 3 * 8
INNER2 = 6 * 8
ROWS2 = INNER2 + 5 * 8
gamma_gas = 1.4
courant = 0.4


def placement():
    fine = np.zeros((256, 512), np.float32)
    coarse = np.zeros((128, 128), np.float32)
    for oy in range(2):
        for oz in range(2):
            for j in range(8):
                for k in range(8):
                    row = oy * 128 + oz * 64 + j * 8 + k
                    lane = (oy * 4 + j // 2) * PITCH + oz * 4 + k // 2
                    fine[row, (j % 2 * 2 + k % 2) * 128 + lane] = 1
    for j in range(8):
        for k in range(8):
            coarse[j * 8 + k, j * PITCH + k] = 1
    return fine, coarse


def place(values, matrix):
    high = values.astype(jnp.bfloat16)
    rest = values - high.astype(jnp.float32)
    middle = rest.astype(jnp.bfloat16)
    low = (rest - middle.astype(jnp.float32)).astype(jnp.bfloat16)
    rows = values.shape[0]
    parts = jnp.concatenate([high, middle, low], axis=0)
    out = jnp.dot(parts, matrix, preferred_element_type=jnp.float32)
    return out[:rows] + out[rows : 2 * rows] + out[2 * rows :]


def roll(x, shift, axis):
    shift = shift % x.shape[axis]
    return pltpu.roll(x, shift, axis) if shift else x


def positions(rows):
    row = lax.broadcasted_iota(jnp.int32, (rows, LANES), 0)
    lane = lax.broadcasted_iota(jnp.int32, (rows, LANES), 1)
    x = jnp.where(row > 8, row - 16, row)
    along = (lane + PITCH + 1) & (LANES - 1)
    y1 = (along * 205) >> 11
    return lane, x, y1 - 1, along - y1 * PITCH - 1


def inside(pos):
    return (pos >= 0) & (pos < 8)


def primitive(u):
    inverse = 1.0 / u[0]
    v = [u[1 + d] * inverse for d in range(3)]
    pressure = 0.4 * (u[4] - 0.5 * (u[1] * v[0] + u[2] * v[1] + u[3] * v[2]))
    sound = jnp.sqrt(gamma_gas * pressure * inverse)
    return v, pressure, sound


def cell_flux(u, prim, d):
    v, pressure, sound = prim
    flux = [u[1 + d]] + [u[1 + e] * v[d] for e in range(3)] + [(u[4] + pressure) * v[d]]
    flux[1 + d] = flux[1 + d] + pressure
    return list(u) + flux + [jnp.abs(v[d]) + sound]


def face(left, right):
    speed = jnp.maximum(left[10], right[10])
    return [(left[5 + f] + right[5 + f]) - speed * (right[f] - left[f]) for f in range(5)]


def ahead(x, d):
    return roll(x, -1, 0) if d == 0 else roll(x, -PITCH if d == 1 else -1, 1)


def behind(x, d):
    return roll(x, 1, 0) if d == 0 else roll(x, PITCH if d == 1 else 1, 1)


def fine_net(u, inner):
    prims = [primitive(u[q]) for q in range(8)]
    total = [None] * 8
    for d in range(3):
        bit = 4 >> d
        cut = (lambda x: x[:8]) if inner and d > 0 else (lambda x: x)
        keep = (lambda x: x[:8]) if inner else (lambda x: x)
        for low in range(8):
            if low & bit:
                continue
            high = low | bit
            cells = []
            for q in (low, high):
                v, pressure, sound = prims[q]
                cells.append(cell_flux([cut(x) for x in u[q]], ([cut(x) for x in v], cut(pressure), cut(sound)), d))
            middle = face(cells[0], cells[1])
            after = face(cells[1], [ahead(x, d) for x in cells[0]])
            net_low = [keep(middle[f] - behind(after[f], d)) for f in range(5)]
            net_high = [keep(after[f] - middle[f]) for f in range(5)]
            for q, net in ((low, net_low), (high, net_high)):
                total[q] = net if total[q] is None else [s + n for s, n in zip(total[q], net)]
    return total


def coarse_net(u, deep, pos):
    prim = primitive(u)
    prim_deep = None if deep is None else primitive(deep)
    total = None
    for d in range(3):
        cell = cell_flux(u, prim, d)
        right = [ahead(x, d) for x in cell]
        if deep is not None:
            outer = cell_flux(deep, prim_deep, d)
            last, first = pos[d] == 8, pos[d] == -1
            right = [jnp.where(last, o, r) for o, r in zip(outer, right)]
        after = face(cell, right)
        before = [behind(x, d) for x in after]
        if deep is not None:
            before = [jnp.where(first, o, b) for o, b in zip(face(outer, cell), before)]
        net = [a - b for a, b in zip(after, before)]
        total = net if total is None else [s + n for s, n in zip(total, net)]
    return total


def prepare(pos_ref, refined_ref, coarse_ref, fine_ref, place_ref, place_coarse_ref, inner_ref, send_ref, scr, scr_c):
    lane, x, y, z = positions(8)
    left_half = lane < 64
    for o in range(8):
        for q in range(4):
            row = (o // 4 * 4 + q) * 8
            scr[o % 4, row : row + 5, :] = fine_ref[o, :, q * 128 : q * 128 + 128]
    for q in range(4):
        tile = coarse_ref[:, q * 128 : q * 128 + 128]
        scr_c[q * 16 : q * 16 + 5, :] = tile
        scr_c[q * 16 + 8 : q * 16 + 13, :] = roll(tile, 64, 1)
    sides = [[], []]
    for f in range(5):
        tile = [scr[c, pl.ds(f, 8, stride=8), :] for c in range(4)]
        sides[0].append(
            jnp.concatenate([jnp.where(left_half, tile[2 * h], roll(tile[2 * h + 1], 64, 1)) for h in range(2)], axis=1)
        )
        sides[1].append(
            jnp.concatenate([jnp.where(left_half, roll(tile[2 * h], 64, 1), tile[2 * h + 1]) for h in range(2)], axis=1)
        )
    fine = place(jnp.concatenate(sides[0] + sides[1], axis=0), place_ref[...])
    coarse = place(jnp.concatenate([scr_c[pl.ds(f, 8, stride=8), :] for f in range(5)], axis=0), place_coarse_ref[...])
    coarse = [coarse[f * 8 : f * 8 + 8] for f in range(5)]

    covered = jnp.zeros((8, LANES), jnp.float32)
    for o in range(8):
        here = ((x >= 4) == (o >= 4)) & ((y >= 4) == (o % 4 >= 2)) & ((z >= 4) == (o % 2 == 1))
        covered = jnp.where(here, (refined_ref[o] > 0).astype(jnp.float32), covered)
    state = []
    for f in range(5):
        for q in range(8):
            row = (q // 4 * 5 + f) * 8
            part = fine[row : row + 8, q % 4 * 128 : q % 4 * 128 + 128]
            state.append(jnp.where(covered > 0.5, part, coarse[f]))
    state += coarse
    fastest = None
    for u in [[state[f * 8 + q] for f in range(5)] for q in range(8)] + [coarse]:
        v, pressure, sound = primitive(u)
        speed = jnp.abs(v[0]) + jnp.abs(v[1]) + jnp.abs(v[2]) + 3.0 * sound
        fastest = speed if fastest is None else jnp.maximum(fastest, speed)
    fastest = jnp.where(inside(y) & inside(z), fastest, 0.0)
    fastest = jnp.broadcast_to(jnp.max(fastest), (1, LANES))

    zero = jnp.zeros((8, LANES), jnp.float32)
    stored = state + [zero] * 5 + [covered]
    for n in range(COUNT):
        inner_ref[n] = stored[n]
    up, down = pos_ref[0], pos_ref[1]
    for t in range(8):
        send_ref[t, COUNT : COUNT + 1, :] = fastest
    for n in range(COUNT):
        deep = DEEP <= n < COVER
        source = stored[n - 5] if deep else stored[n]
        high, low = (6, 1) if deep else (7, 0)
        send_ref[up, n : n + 1, :] = source[high : high + 1, :]
        send_ref[down, n : n + 1, :] = source[low : low + 1, :]


def forward_y(pos_ref, got_ref, inner_ref, outer_ref, send_ref):
    lane, x, y, z = positions(8)
    row = lax.broadcasted_iota(jnp.int32, (8, LANES), 0)
    up, down = pos_ref[0], pos_ref[1]
    fastest = got_ref[0, COUNT : COUNT + 1, :]
    for t in range(1, 8):
        fastest = jnp.maximum(fastest, got_ref[t, COUNT : COUNT + 1, :])
    fastest = jnp.broadcast_to(fastest, (8, LANES))
    for n in range(COUNT):
        above = jnp.broadcast_to(got_ref[up, n : n + 1, :], (8, LANES))
        below = jnp.broadcast_to(got_ref[down, n : n + 1, :], (8, LANES))
        outer_ref[n] = jnp.where(row == 0, above, jnp.where(row == 7, below, 0.0))
    for t in range(8):
        send_ref[t, INNER1 - 8 : INNER1, :] = fastest
    up, down = pos_ref[2], pos_ref[3]
    for slot, at, deep_at in ((up, 7, 6), (down, 0, 1)):
        for first, source, count in ((0, inner_ref, COUNT), (INNER1, outer_ref, DEEP)):
            for block in range((count + 15) // 16):
                packed = fastest
                for s in range(16):
                    n = block * 16 + s
                    if n >= count:
                        break
                    deep = DEEP <= n < COVER
                    value = source[n - 5 if deep else n]
                    value = roll(value, s * 8 - (deep_at if deep else at) * PITCH, 1)
                    packed = jnp.where((lane >> 3) == s, value, packed)
                send_ref[slot, first + block * 8 : first + block * 8 + 8, :] = packed


def forward_z(pos_ref, got_ref, inner_ref, outer_ref, inner_out, outer_out, send_ref):
    lane, x, y, z = positions(8)
    up, down = pos_ref[2], pos_ref[3]
    fastest = got_ref[0, INNER1 - 8 : INNER1, :]
    for t in range(1, 8):
        fastest = jnp.maximum(fastest, got_ref[t, INNER1 - 8 : INNER1, :])
    below_lanes = (lane >= LANES - PITCH) & (lane < LANES - PITCH + 8)
    above_lanes = (lane >= 8 * PITCH) & (lane < 8 * PITCH + 8)
    for first, source, target, count in ((0, inner_ref, inner_out, COUNT), (INNER1, outer_ref, outer_out, DEEP)):
        for n in range(COUNT):
            value = source[n]
            if n < count:
                block, s = n // 16, n % 16
                below = got_ref[down, first + block * 8 : first + block * 8 + 8, :]
                above = got_ref[up, first + block * 8 : first + block * 8 + 8, :]
                value = jnp.where(below_lanes, roll(below, -PITCH - s * 8, 1), value)
                value = jnp.where(above_lanes, roll(above, 8 * PITCH - s * 8, 1), value)
            target[n] = value
    for t in range(8):
        send_ref[t, 0:8, :] = fastest
    up, down = pos_ref[4], pos_ref[5]
    along = (lane + PITCH) & (LANES - 1)
    slots = along - ((along * 205) >> 11) * PITCH
    slots = jnp.where(along < 10 * PITCH, slots, -1)
    for slot, at, deep_at in ((up, 7, 6), (down, 0, 1)):
        for first, source, count in ((0, inner_out, COUNT), (INNER2, outer_out, DEEP)):
            for block in range((count + 9) // 10):
                packed = fastest
                for s in range(10):
                    n = block * 10 + s
                    if n >= count:
                        break
                    deep = DEEP <= n < COVER
                    value = roll(source[n - 5 if deep else n], s - (deep_at if deep else at), 1)
                    packed = jnp.where(slots == s, value, packed)
                send_ref[slot, first + block * 8 : first + block * 8 + 8, :] = packed


def advance(
    pos_ref, got_ref, inner_ref, outer_ref, back_ref, back_coarse_ref, coarse_out, fine_out, scr, scr_c
):
    lane, x, y, z = positions(16)
    up, down = pos_ref[4], pos_ref[5]
    fastest = got_ref[0, 0:8, :]
    for t in range(1, 8):
        fastest = jnp.maximum(fastest, got_ref[t, 0:8, :])
    fastest = jnp.where((lane[:8] >= 90) & (lane[:8] < 118), fastest, 0.0)
    fastest = jnp.broadcast_to(jnp.max(fastest), (8, LANES))
    half = 0.5 * (courant / fastest)
    half16 = jnp.concatenate([half, half], axis=0)

    below_lanes, above_lanes = z[:8] == -1, z[:8] == 8
    state = []
    for n in range(COUNT):
        parts = []
        for first, source, count in ((0, inner_ref, COUNT), (INNER2, outer_ref, DEEP)):
            value = source[n]
            if n < count:
                block, s = n // 10, n % 10
                below = got_ref[down, first + block * 8 : first + block * 8 + 8, :]
                above = got_ref[up, first + block * 8 : first + block * 8 + 8, :]
                value = jnp.where(below_lanes, roll(below, -1 - s, 1), value)
                value = jnp.where(above_lanes, roll(above, 8 - s, 1), value)
            parts.append(value)
        state.append(jnp.concatenate(parts, axis=0))
    covered = state[COVER] > 0.5
    fine0 = [[state[f * 8 + q] for f in range(5)] for q in range(8)]
    coarse0 = state[COARSE:DEEP]

    net = coarse_net(coarse0, state[DEEP:COVER], (x, y, z))
    coarse1 = [u - 0.5 * half16 * n for u, n in zip(coarse0, net)]
    net = fine_net(fine0, False)
    fine1 = [
        [jnp.where(covered, fine0[q][f] - half16 * net[q][f], coarse1[f]) for f in range(5)] for q in range(8)
    ]
    net = coarse_net(coarse1, None, None)
    coarse2 = [0.5 * c0[:8] + 0.5 * (c1[:8] - 0.5 * half * n[:8]) for c0, c1, n in zip(coarse0, coarse1, net)]
    net = fine_net(fine1, True)
    mine = inside(y[:8]) & inside(z[:8])
    refined = mine & covered[:8]
    fine2 = [
        [
            jnp.where(refined, 0.5 * fine0[q][f][:8] + 0.5 * (fine1[q][f][:8] - half * net[q][f]), 0.0)
            for f in range(5)
        ]
        for q in range(8)
    ]
    coarse = []
    for f in range(5):
        total = functools.reduce(jnp.add, [fine2[q][f] for q in range(8)])
        coarse.append(jnp.where(mine, jnp.where(refined, 0.125 * total, coarse2[f]), 0.0))

    left_half = lane[:8] < 64
    rows = [jnp.concatenate([fine2[a * 4 + q][f] for q in range(4)], axis=1) for a in range(2) for f in range(5)]
    back = place(jnp.concatenate(rows, axis=0), back_ref[...])
    for f in range(5):
        for h in range(2):
            even = back[f * 8 : f * 8 + 8, h * 128 : h * 128 + 128]
            odd = back[40 + f * 8 : 48 + f * 8, h * 128 : h * 128 + 128]
            scr[2 * h, pl.ds(f, 8, stride=8), :] = jnp.where(left_half, even, roll(odd, 64, 1))
            scr[2 * h + 1, pl.ds(f, 8, stride=8), :] = jnp.where(left_half, roll(even, 64, 1), odd)
    for o in range(8):
        for q in range(4):
            row = (o // 4 * 4 + q) * 8
            fine_out[o, :, q * 128 : q * 128 + 128] = scr[o % 4, row : row + 5, :]
    back = place(jnp.concatenate(coarse, axis=0), back_coarse_ref[...])
    for f in range(5):
        scr_c[pl.ds(f, 8, stride=8), :] = back[f * 8 : f * 8 + 8]
    for q in range(4):
        even = scr_c[q * 16 : q * 16 + 5, :]
        odd = scr_c[q * 16 + 8 : q * 16 + 13, :]
        coarse_out[:, q * 128 : q * 128 + 128] = jnp.where(left_half[:5], even, roll(odd, 64, 1))


def shape(*dims):
    return jax.ShapeDtypeStruct(dims, jnp.float32)


def call(kernel, kinds, outs, scratch, args):
    spaces = {"s": pltpu.SMEM, "v": pltpu.VMEM}
    return pl.pallas_call(
        kernel,
        out_shape=outs,
        in_specs=[pl.BlockSpec(memory_space=spaces[k]) for k in kinds],
        out_specs=[pl.BlockSpec(memory_space=pltpu.VMEM)] * len(outs),
        scratch_shapes=scratch,
        compiler_params=pltpu.CompilerParams(vmem_limit_bytes=32 * 1024 * 1024),
    )(*args)


def lines(count, dim):
    bits = count.bit_length() - 1
    mask = sum(1 << t for t in range(bits) if t % 3 == dim)
    groups = {}
    for device in range(count):
        groups.setdefault(device & ~mask, []).append(device)
    return list(groups.values())


def swap(block, dim):
    return lax.all_to_all(block, "boxes", 0, 0, axis_index_groups=lines(lax.axis_size("boxes"), dim))


def local(coarse_state, fine_state, refined):
    fine_place, coarse_place = placement()
    as_matrix = lambda m: jnp.asarray(np.ascontiguousarray(m).astype(ml_dtypes.bfloat16))
    device = lax.axis_index("boxes")
    pos = []
    for dim in range(3):
        here = sum(((device >> (3 * i + dim)) & 1) << i for i in range(3))
        pos += [(here + 1) & 7, (here + 7) & 7]
    pos = jnp.stack(pos).astype(jnp.int32)
    scratch = [pltpu.VMEM((4, 64, LANES), jnp.float32), pltpu.VMEM((64, LANES), jnp.float32)]
    field = shape(COUNT, 8, LANES)

    inner, send = call(
        prepare,
        "ssvvvv",
        [field, shape(8, ROWS0, LANES)],
        scratch,
        (pos, refined[0], coarse_state[0], fine_state[0], as_matrix(fine_place), as_matrix(coarse_place)),
    )
    got = swap(send, 0)
    outer, send = call(forward_y, "svv", [field, shape(8, ROWS1, LANES)], [], (pos, got, inner))
    got = swap(send, 1)
    inner, outer, send = call(
        forward_z, "svvv", [field, field, shape(8, ROWS2, LANES)], [], (pos, got, inner, outer)
    )
    got = swap(send, 2)
    coarse_out, fine_out = call(
        advance,
        "svvvvv",
        [shape(5, 512), shape(8, 5, 512)],
        scratch,
        (pos, got, inner, outer, as_matrix(fine_place.T), as_matrix(coarse_place.T)),
    )
    return coarse_out[None], fine_out[None]


def solution(mesh):
    in_specs = (P("boxes", None, None), P("boxes", None, None, None), P("boxes", None))
    out_specs = (P("boxes", None, None), P("boxes", None, None, None))
    return jax.shard_map(local, mesh=mesh, in_specs=in_specs, out_specs=out_specs, check_vma=False)
```

profile of v0, /device:TPU:32, one launch (start us, length us, event | category | flops | bytes accessed | tf_op | source)
XLA Modules:
  0.0 84.2 jit_solution(17530344322409193323)
XLA Ops:
  0.6 0.0 copy-start
  0.7 0.7 copy.16
  1.4 0.0 copy-start.3
  1.4 0.9 %copy.15 = f32[1,8,5,512]{3,2,1,0:T(8,128)S(1)} copy(f32[1,8,5,512]{3,1,2,0:T(8,128)} %param.8) | data formatting | bytes 163840 | tf_op args[1]
  2.4 0.1 stack.27.pos_ref
  2.4 0.0 copy-start.4
  2.5 0.0 copy-done
  2.5 0.0 copy-done.3
  2.5 0.6 copy-done.4
  3.1 1.1 %shard_map.86 = (f32[51,8,128]{2,1,0:T(8,128)S(1)}, f32[8,56,128]{2,1,0:T(8,128)S(1)}) custom-call(s32[6]{0:T(128)S(1)} %stack.27.pos_ref, s32[8]{0:T(128)S(1)} %bitcast.19, f32[5,512]{1,0:T(8,128)S(1)} %bitcast.17, f32[8,5,512]{2,1,0:T(8,128)S(1)} %bitcast.15, bf16[256,512]{1,0:T(8,128)(2,1)S(1)} %copy-done, bf16[128,128]{1,0:T(8,128)(2,1)S(1)} %copy-done.3), custom_call_target="tpu_custom_call" | custom-call | tf_op jit(solution)/shard_map/pallas_call | solution.py:353
  4.2 12.1 %all_to_all.15.got_ref = f32[8,56,128]{2,1,0:T(8,128)S(1)} all-to-all(f32[8,56,128]{2,1,0:T(8,128)S(1)} %get-tuple-element.11), channel_id=1, replica_groups={{0,1,8,9,64,65,72,73},{2,3,10,11,66,67,74,75},{4,5,12,13,68,69,76,77},{..., dimensions={0} | all-to-all | bytes 458752 | tf_op jit(solution)/shard_map/all_to_all | solution.py:373
  16.2 0.8 shard_map.87
  17.0 27.7 %all_to_all.16.got_ref = f32[8,56,128]{2,1,0:T(8,128)S(1)} all-to-all(f32[8,56,128]{2,1,0:T(8,128)S(1)} %get-tuple-element.13), channel_id=1, replica_groups={{0,2,16,18,128,130,144,146},{1,3,17,19,129,131,145,147},{4,6,20,22,132,..., dimensions={0} | all-to-all | bytes 458752 | tf_op jit(solution)/shard_map/all_to_all | solution.py:373
  44.8 1.0 %shard_map.88 = (f32[51,8,128]{2,1,0:T(8,128)S(1)}, f32[51,8,128]{2,1,0:T(8,128)S(1)}, f32[8,88,128]{2,1,0:T(8,128)S(1)}) custom-call(s32[6]{0:T(128)S(1)} %stack.27.pos_ref, f32[8,56,128]{2,1,0:T(8,128)S(1)} %all_to_all.16.got_ref, f32[51,8,128]{2,1,0:T(8,128)S(1)} %get-tuple-element.12.inner_ref, f32[51,8,128]{2,1,0:T(8,128)S(1)} %get-tuple-element.14.outer_ref), custom_call_target="tpu_custom_call" | custom-call | tf_op jit(solution)/shard_map/pallas_call | solution.py:353
  45.7 0.0 copy-start.1
  45.8 0.0 copy-start.2
  45.8 35.0 %all_to_all.17.got_ref = f32[8,88,128]{2,1,0:T(8,128)S(1)} all-to-all(f32[8,88,128]{2,1,0:T(8,128)S(1)} %get-tuple-element.15), channel_id=1, replica_groups={{0,4,32,36,256,260,288,292},{1,5,33,37,257,261,289,293},{2,6,34,38,258,..., dimensions={0} | all-to-all | bytes 720896 | tf_op jit(solution)/shard_map/all_to_all | solution.py:373
  80.8 0.0 copy-done.1
  80.8 0.0 copy-done.2
  80.8 2.0 %shard_map.89 = (f32[5,512]{1,0:T(8,128)S(1)}, f32[8,5,512]{2,1,0:T(8,128)S(1)}) custom-call(s32[6]{0:T(128)S(1)} %stack.27.pos_ref, f32[8,88,128]{2,1,0:T(8,128)S(1)} %all_to_all.17.got_ref, f32[51,8,128]{2,1,0:T(8,128)S(1)} %get-tuple-element.16.inner_ref, f32[51,8,128]{2,1,0:T(8,128)S(1)} %get-tuple-element.17.outer_ref, bf16[512,256]{1,0:T(8,128)(2,1)S(1)} %copy-done.1, ...), custom_call_target="tpu_custom_call" | custom-call | tf_op jit(solution)/shard_map/pallas_call | solution.py:353
  82.9 0.6 copy.10
  83.5 0.7 copy.11
Async XLA Ops:
  0.6 1.8 %copy-start = (bf16[256,512]{1,0:T(8,128)(2,1)S(1)}, bf16[256,512]{1,0:T(8,128)(2,1)}, u32[]{:S(2)}) copy-start(bf16[256,512]{1,0:T(8,128)(2,1)} %constant.30.clone.place_ref) | copy-start | bytes 786436
  1.4 1.0 %copy-start.3 = (bf16[128,128]{1,0:T(8,128)(2,1)S(1)}, bf16[128,128]{1,0:T(8,128)(2,1)}, u32[]{:S(2)}) copy-start(bf16[128,128]{1,0:T(8,128)(2,1)} %constant.31.clone.place_coarse_ref) | copy-start | bytes 98308
  2.4 0.7 copy-start.4
  45.7 35.1 %copy-start.1 = (bf16[512,256]{1,0:T(8,128)(2,1)S(1)}, bf16[512,256]{1,0:T(8,128)(2,1)}, u32[]{:S(2)}) copy-start(bf16[512,256]{1,0:T(8,128)(2,1)} %constant.32.clone.back_ref) | copy-start | bytes 786436
  45.8 35.1 %copy-start.2 = (bf16[128,128]{1,0:T(8,128)(2,1)S(1)}, bf16[128,128]{1,0:T(8,128)(2,1)}, u32[]{:S(2)}) copy-start(bf16[128,128]{1,0:T(8,128)(2,1)} %constant.33.clone.back_coarse_ref) | copy-start | bytes 98308
where the time goes:
time: 84.4 us; the launch traced here: 84.2 us
  blocking collectives  74.8 us (89%)
  Pallas kernels  4.89 us (6%)
  local copies, waits for them, and re-layouts  3.75 us (4%)
    all_to_all x3, blocking collectives, swap(): lax.all_to_all(block, 'boxes', 0, 0, axis_index_groups=lines(lax.axis_siz...  74.8 us
    pallas_call x4, Pallas kernels, call(): pl.pallas_call(kernel, out_shape=outs, in_specs=[pl.BlockSpec(memory_spac...  4.89 us
    unnamed x14, local copies, waits for them, and re-layouts  3.66 us

commit v1 on v0

--- a/solution.py
+++ b/solution.py
@@ -16,11 +16,10 @@
 DEEP = COARSE + 5
 COVER = DEEP + 5
 COUNT = COVER + 1
-ROWS0 = 56
-INNER1 = 4 * 8
-ROWS1 = INNER1 + 3 * 8
-INNER2 = 6 * 8
-ROWS2 = INNER2 + 5 * 8
+WHOLE = 34
+ROWS0 = 40
+ROWS1 = 32
+ROWS2 = 32
 gamma_gas = 1.4
 courant = 0.4
 
@@ -142,28 +141,68 @@
     return total
 
 
+def rows_of(fields):
+    row = lax.broadcasted_iota(jnp.int32, (8, LANES), 0)
+    merged = []
+    for j in range(0, len(fields), 4):
+        packed = fields[j]
+        for i, value in enumerate(fields[j : j + 4]):
+            if i:
+                here = (row == 2 * i) | (row == 2 * i - 1)
+                packed = jnp.where(here, roll(value, 2 * i, 0), packed)
+        merged.append(packed)
+    return merged
+
+
+def edge_fields(outer, fixed_bit, at_high):
+    row = lax.broadcasted_iota(jnp.int32, (8, LANES), 0)
+    fields = []
+    for f in range(5):
+        for other in range(2):
+            q = (fixed_bit if at_high else 0) + (3 - fixed_bit) * other
+            fields.append(jnp.where(row == 0, outer(f * 8 + q), outer(f * 8 + 4 + q)))
+    return fields + [outer(COARSE + f) for f in range(5)]
+
+
+def edge_targets(fixed_bit, from_below):
+    targets = []
+    for f in range(5):
+        for other in range(2):
+            q = (fixed_bit if from_below else 0) + (3 - fixed_bit) * other
+            targets.append([f * 8 + q, f * 8 + 4 + q])
+    return targets + [[COARSE + f] for f in range(5)]
+
+
+def is_deep(n):
+    return DEEP <= n < COVER
+
+
 def prepare(pos_ref, refined_ref, coarse_ref, fine_ref, place_ref, place_coarse_ref, inner_ref, send_ref, scr, scr_c):
     lane, x, y, z = positions(8)
+    row = lax.broadcasted_iota(jnp.int32, (8, LANES), 0)
     left_half = lane < 64
-    for o in range(8):
+    for f in range(5):
         for q in range(4):
-            row = (o // 4 * 4 + q) * 8
-            scr[o % 4, row : row + 5, :] = fine_ref[o, :, q * 128 : q * 128 + 128]
-    for q in range(4):
-        tile = coarse_ref[:, q * 128 : q * 128 + 128]
-        scr_c[q * 16 : q * 16 + 5, :] = tile
-        scr_c[q * 16 + 8 : q * 16 + 13, :] = roll(tile, 64, 1)
+            tile = fine_ref[f, :, q * 128 : q * 128 + 128]
+            for ox in range(2):
+                scr[f, pl.ds(ox * 4 + q, 4, stride=8), :] = tile[ox * 4 : ox * 4 + 4]
+            part = coarse_ref[f, :, q * 128 : q * 128 + 128]
+            scr_c[f, 2 * q : 2 * q + 1, :] = part
+            scr_c[f, 2 * q + 1 : 2 * q + 2, :] = part
     sides = [[], []]
-    for f in range(5):
-        tile = [scr[c, pl.ds(f, 8, stride=8), :] for c in range(4)]
+    rows = []
+    for f in range(5):
+        tile = [scr[f, c * 8 : c * 8 + 8, :] for c in range(4)]
         sides[0].append(
             jnp.concatenate([jnp.where(left_half, tile[2 * h], roll(tile[2 * h + 1], 64, 1)) for h in range(2)], axis=1)
         )
         sides[1].append(
             jnp.concatenate([jnp.where(left_half, roll(tile[2 * h], 64, 1), tile[2 * h + 1]) for h in range(2)], axis=1)
         )
+        value = scr_c[f]
+        rows.append(jnp.where((row & 1) == 1, roll(value, 64, 1), value))
     fine = place(jnp.concatenate(sides[0] + sides[1], axis=0), place_ref[...])
-    coarse = place(jnp.concatenate([scr_c[pl.ds(f, 8, stride=8), :] for f in range(5)], axis=0), place_coarse_ref[...])
+    coarse = place(jnp.concatenate(rows, axis=0), place_coarse_ref[...])
     coarse = [coarse[f * 8 : f * 8 + 8] for f in range(5)]
 
     covered = jnp.zeros((8, LANES), jnp.float32)
@@ -173,8 +212,8 @@
     state = []
     for f in range(5):
         for q in range(8):
-            row = (q // 4 * 5 + f) * 8
-            part = fine[row : row + 8, q % 4 * 128 : q % 4 * 128 + 128]
+            first = (q // 4 * 5 + f) * 8
+            part = fine[first : first + 8, q % 4 * 128 : q % 4 * 128 + 128]
             state.append(jnp.where(covered > 0.5, part, coarse[f]))
     state += coarse
     fastest = None
@@ -189,112 +228,153 @@
     stored = state + [zero] * 5 + [covered]
     for n in range(COUNT):
         inner_ref[n] = stored[n]
-    up, down = pos_ref[0], pos_ref[1]
     for t in range(8):
-        send_ref[t, COUNT : COUNT + 1, :] = fastest
-    for n in range(COUNT):
-        deep = DEEP <= n < COVER
-        source = stored[n - 5] if deep else stored[n]
-        high, low = (6, 1) if deep else (7, 0)
-        send_ref[up, n : n + 1, :] = source[high : high + 1, :]
-        send_ref[down, n : n + 1, :] = source[low : low + 1, :]
+        send_ref[t, WHOLE : WHOLE + 1, :] = fastest
+    for slot, at, step in ((pos_ref[0], 7, 1), (pos_ref[1], 0, -1)):
+        for n in range(WHOLE):
+            m = WHOLE + n // 2
+            half = roll(stored[m - 5], step, 0) if is_deep(m) else stored[m]
+            packed = jnp.where(lane < 80, stored[n], roll(half, 40 if n % 2 else 80, 1))
+            send_ref[slot, n : n + 1, :] = packed[at : at + 1, :]
 
 
 def forward_y(pos_ref, got_ref, inner_ref, outer_ref, send_ref):
     lane, x, y, z = positions(8)
     row = lax.broadcasted_iota(jnp.int32, (8, LANES), 0)
     up, down = pos_ref[0], pos_ref[1]
-    fastest = got_ref[0, COUNT : COUNT + 1, :]
+    fastest = got_ref[0, WHOLE : WHOLE + 1, :]
     for t in range(1, 8):
-        fastest = jnp.maximum(fastest, got_ref[t, COUNT : COUNT + 1, :])
+        fastest = jnp.maximum(fastest, got_ref[t, WHOLE : WHOLE + 1, :])
     fastest = jnp.broadcast_to(fastest, (8, LANES))
-    for n in range(COUNT):
+    outer = []
+    for n in range(WHOLE):
         above = jnp.broadcast_to(got_ref[up, n : n + 1, :], (8, LANES))
         below = jnp.broadcast_to(got_ref[down, n : n + 1, :], (8, LANES))
-        outer_ref[n] = jnp.where(row == 0, above, jnp.where(row == 7, below, 0.0))
+        outer.append(jnp.where(row == 0, above, below))
+    for n in range(0, WHOLE, 2):
+        outer.append(jnp.where(lane < 40, roll(outer[n], -80, 1), roll(outer[n + 1], -40, 1)))
+    for n in range(COUNT):
+        outer_ref[n] = outer[n]
     for t in range(8):
-        send_ref[t, INNER1 - 8 : INNER1, :] = fastest
-    up, down = pos_ref[2], pos_ref[3]
-    for slot, at, deep_at in ((up, 7, 6), (down, 0, 1)):
-        for first, source, count in ((0, inner_ref, COUNT), (INNER1, outer_ref, DEEP)):
-            for block in range((count + 15) // 16):
-                packed = fastest
-                for s in range(16):
-                    n = block * 16 + s
-                    if n >= count:
-                        break
-                    deep = DEEP <= n < COVER
-                    value = source[n - 5 if deep else n]
-                    value = roll(value, s * 8 - (deep_at if deep else at) * PITCH, 1)
-                    packed = jnp.where((lane >> 3) == s, value, packed)
-                send_ref[slot, first + block * 8 : first + block * 8 + 8, :] = packed
+        send_ref[t, ROWS1 - 8 : ROWS1, :] = fastest
+    for slot, at, deep_at in ((pos_ref[2], 7, 6), (pos_ref[3], 0, 1)):
+        items = [(inner_ref[n - 5], deep_at) if is_deep(n) else (inner_ref[n], at) for n in range(COUNT)]
+        items += [(value, at) for value in rows_of(edge_fields(lambda n: outer[n], 2, at == 7))]
+        for block in range(4):
+            packed = fastest
+            for s, (value, where) in enumerate(items[block * 16 : block * 16 + 16]):
+                packed = jnp.where((lane >> 3) == s, roll(value, s * 8 - where * PITCH, 1), packed)
+            send_ref[slot, block * 8 : block * 8 + 8, :] = packed
 
 
 def forward_z(pos_ref, got_ref, inner_ref, outer_ref, inner_out, outer_out, send_ref):
     lane, x, y, z = positions(8)
-    up, down = pos_ref[2], pos_ref[3]
-    fastest = got_ref[0, INNER1 - 8 : INNER1, :]
+    fastest = got_ref[0, ROWS1 - 8 : ROWS1, :]
     for t in range(1, 8):
-        fastest = jnp.maximum(fastest, got_ref[t, INNER1 - 8 : INNER1, :])
-    below_lanes = (lane >= LANES - PITCH) & (lane < LANES - PITCH + 8)
-    above_lanes = (lane >= 8 * PITCH) & (lane < 8 * PITCH + 8)
-    for first, source, target, count in ((0, inner_ref, inner_out, COUNT), (INNER1, outer_ref, outer_out, DEEP)):
+        fastest = jnp.maximum(fastest, got_ref[t, ROWS1 - 8 : ROWS1, :])
+    inner = [inner_ref[n] for n in range(COUNT)]
+    outer = [outer_ref[n] for n in range(COUNT)]
+    for slot, at, from_below in ((pos_ref[3], -1, True), (pos_ref[2], 8, False)):
+        first = at * PITCH % LANES
+        here = (lane >= first) & (lane < first + 8)
         for n in range(COUNT):
-            value = source[n]
-            if n < count:
-                block, s = n // 16, n % 16
-                below = got_ref[down, first + block * 8 : first + block * 8 + 8, :]
-                above = got_ref[up, first + block * 8 : first + block * 8 + 8, :]
-                value = jnp.where(below_lanes, roll(below, -PITCH - s * 8, 1), value)
-                value = jnp.where(above_lanes, roll(above, 8 * PITCH - s * 8, 1), value)
-            target[n] = value
+            block, s = n // 16, n % 16
+            value = got_ref[slot, block * 8 : block * 8 + 8, :]
+            inner[n] = jnp.where(here, roll(value, first - s * 8, 1), inner[n])
+        targets = edge_targets(2, from_below)
+        for j in range(4):
+            merged = roll(got_ref[slot, 24:32, :], first - (COUNT % 16 + j) * 8, 1)
+            for i, names in enumerate(targets[4 * j : 4 * j + 4]):
+                value = roll(merged, -2 * i, 0)
+                for n in names:
+                    outer[n] = jnp.where(here, value, outer[n])
+    for n in range(COUNT):
+        inner_out[n] = inner[n]
+        outer_out[n] = outer[n]
+
     for t in range(8):
-        send_ref[t, 0:8, :] = fastest
-    up, down = pos_ref[4], pos_ref[5]
-    along = (lane + PITCH) & (LANES - 1)
-    slots = along - ((along * 205) >> 11) * PITCH
-    slots = jnp.where(along < 10 * PITCH, slots, -1)
-    for slot, at, deep_at in ((up, 7, 6), (down, 0, 1)):
-        for first, source, count in ((0, inner_out, COUNT), (INNER2, outer_out, DEEP)):
-            for block in range((count + 9) // 10):
-                packed = fastest
-                for s in range(10):
-                    n = block * 10 + s
-                    if n >= count:
-                        break
-                    deep = DEEP <= n < COVER
-                    value = roll(source[n - 5 if deep else n], s - (deep_at if deep else at), 1)
-                    packed = jnp.where(slots == s, value, packed)
-                send_ref[slot, first + block * 8 : first + block * 8 + 8, :] = packed
+        send_ref[t, ROWS2 - 8 : ROWS2, :] = fastest
+    along = (lane * 205) >> 11
+    slots = lane - along * PITCH
+    for slot, at, deep_at in ((pos_ref[4], 7, 6), (pos_ref[5], 0, 1)):
+        high = at == 7
+        halves = []
+        for n in range(FINE, COUNT):
+            value, where = (inner[n - 5], deep_at) if is_deep(n) else (inner[n], at)
+            halves += [(value, 80 - where), (value, 40 - where)]
+        for value in rows_of(edge_fields(lambda n: outer[n], 1, high)):
+            halves += [(value, 80 - at), (value, 40 - at)]
+        columns = []
+        for f in range(5):
+            for a in range(2):
+                q = a * 4 + high
+                columns += [(inner[f * 8 + q + 2], at - PITCH), (inner[f * 8 + q], at + 8 * PITCH)]
+        for f in range(5):
+            columns += [(inner[COARSE + f], at - PITCH), (inner[COARSE + f], at + 8 * PITCH)]
+        for block in range(4):
+            packed = fastest
+            for s in range(10):
+                packed = jnp.where((slots == s) & (lane < 80), roll(inner[block * 10 + s], s - at, 1), packed)
+            for s, (value, shift) in enumerate(halves[block * 10 : block * 10 + 10]):
+                here = (slots == s) & (lane >= 80) & (lane < 120)
+                packed = jnp.where(here, roll(value, shift + s, 1), packed)
+            for s, (value, place_) in enumerate(columns[block * 8 : block * 8 + 8]):
+                packed = jnp.where(lane == 120 + s, roll(value, 120 + s - place_, 1), packed)
+            send_ref[slot, block * 8 : block * 8 + 8, :] = packed
+
+
+def take_z(pos_ref, got_ref, inner_ref, outer_ref):
+    lane, x, y, z = positions(8)
+    inner = [inner_ref[n] for n in range(COUNT)]
+    outer = [outer_ref[n] for n in range(COUNT)]
+    for slot, at, from_below in ((pos_ref[5], -1, True), (pos_ref[4], 8, False)):
+        got = [got_ref[slot, block * 8 : block * 8 + 8, :] for block in range(4)]
+        here = (z == at) & inside(y)
+        low = here & (y < 4)
+        for n in range(FINE):
+            inner[n] = jnp.where(here, roll(got[n // 10], at - n % 10, 1), inner[n])
+
+        def whole(h):
+            first = roll(got[h // 10], at - 80 - h % 10, 1)
+            second = roll(got[(h + 1) // 10], at - 40 - (h + 1) % 10, 1)
+            return jnp.where(low, first, second)
+
+        for n in range(FINE, COUNT):
+            inner[n] = jnp.where(here, whole(2 * (n - FINE)), inner[n])
+        targets = edge_targets(1, from_below)
+        for j in range(4):
+            merged = whole(2 * (COUNT - FINE) + 2 * j)
+            for i, names in enumerate(targets[4 * j : 4 * j + 4]):
+                value = roll(merged, -2 * i, 0)
+                for n in names:
+                    outer[n] = jnp.where(here, value, outer[n])
+        columns = []
+        for f in range(5):
+            for a in range(2):
+                q = a * 4 + from_below
+                columns += [(f * 8 + q + 2, -1), (f * 8 + q, 8)]
+        for f in range(5):
+            columns += [(COARSE + f, -1), (COARSE + f, 8)]
+        for k, (n, side) in enumerate(columns):
+            target = side * PITCH + at
+            value = roll(got[k // 8], target - (120 + k % 8), 1)
+            inner[n] = jnp.where(lane == target % LANES, value, inner[n])
+    return [jnp.concatenate([i, o], axis=0) for i, o in zip(inner, outer)]
 
 
 def advance(
     pos_ref, got_ref, inner_ref, outer_ref, back_ref, back_coarse_ref, coarse_out, fine_out, scr, scr_c
 ):
     lane, x, y, z = positions(16)
-    up, down = pos_ref[4], pos_ref[5]
-    fastest = got_ref[0, 0:8, :]
+    fastest = got_ref[0, ROWS2 - 8 : ROWS2, :]
     for t in range(1, 8):
-        fastest = jnp.maximum(fastest, got_ref[t, 0:8, :])
-    fastest = jnp.where((lane[:8] >= 90) & (lane[:8] < 118), fastest, 0.0)
+        fastest = jnp.maximum(fastest, got_ref[t, ROWS2 - 8 : ROWS2, :])
+    fastest = jnp.where((lane[:8] >= 80) & (lane[:8] < 120), fastest, 0.0)
     fastest = jnp.broadcast_to(jnp.max(fastest), (8, LANES))
     half = 0.5 * (courant / fastest)
     half16 = jnp.concatenate([half, half], axis=0)
 
-    below_lanes, above_lanes = z[:8] == -1, z[:8] == 8
-    state = []
-    for n in range(COUNT):
-        parts = []
-        for first, source, count in ((0, inner_ref, COUNT), (INNER2, outer_ref, DEEP)):
-            value = source[n]
-            if n < count:
-                block, s = n // 10, n % 10
-                below = got_ref[down, first + block * 8 : first + block * 8 + 8, :]
-                above = got_ref[up, first + block * 8 : first + block * 8 + 8, :]
-                value = jnp.where(below_lanes, roll(below, -1 - s, 1), value)
-                value = jnp.where(above_lanes, roll(above, 8 - s, 1), value)
-            parts.append(value)
-        state.append(jnp.concatenate(parts, axis=0))
+    state = take_z(pos_ref, got_ref, inner_ref, outer_ref)
     covered = state[COVER] > 0.5
     fine0 = [[state[f * 8 + q] for f in range(5)] for q in range(8)]
     coarse0 = state[COARSE:DEEP]
@@ -329,19 +409,18 @@
         for h in range(2):
             even = back[f * 8 : f * 8 + 8, h * 128 : h * 128 + 128]
             odd = back[40 + f * 8 : 48 + f * 8, h * 128 : h * 128 + 128]
-            scr[2 * h, pl.ds(f, 8, stride=8), :] = jnp.where(left_half, even, roll(odd, 64, 1))
-            scr[2 * h + 1, pl.ds(f, 8, stride=8), :] = jnp.where(left_half, roll(even, 64, 1), odd)
-    for o in range(8):
+            scr[f, h * 16 : h * 16 + 8, :] = jnp.where(left_half, even, roll(odd, 64, 1))
+            scr[f, h * 16 + 8 : h * 16 + 16, :] = jnp.where(left_half, roll(even, 64, 1), odd)
         for q in range(4):
-            row = (o // 4 * 4 + q) * 8
-            fine_out[o, :, q * 128 : q * 128 + 128] = scr[o % 4, row : row + 5, :]
+            for ox in range(2):
+                tile = scr[f, pl.ds(ox * 4 + q, 4, stride=8), :]
+                fine_out[f, ox * 4 : ox * 4 + 4, q * 128 : q * 128 + 128] = tile
     back = place(jnp.concatenate(coarse, axis=0), back_coarse_ref[...])
     for f in range(5):
-        scr_c[pl.ds(f, 8, stride=8), :] = back[f * 8 : f * 8 + 8]
-    for q in range(4):
-        even = scr_c[q * 16 : q * 16 + 5, :]
-        odd = scr_c[q * 16 + 8 : q * 16 + 13, :]
-        coarse_out[:, q * 128 : q * 128 + 128] = jnp.where(left_half[:5], even, roll(odd, 64, 1))
+        value = back[f * 8 : f * 8 + 8]
+        value = jnp.where(left_half, value, roll(roll(value, 64, 1), -1, 0))
+        for q in range(4):
+            coarse_out[f, :, q * 128 : q * 128 + 128] = value[2 * q : 2 * q + 1]
 
 
 def shape(*dims):
@@ -382,7 +461,7 @@
         here = sum(((device >> (3 * i + dim)) & 1) << i for i in range(3))
         pos += [(here + 1) & 7, (here + 7) & 7]
     pos = jnp.stack(pos).astype(jnp.int32)
-    scratch = [pltpu.VMEM((4, 64, LANES), jnp.float32), pltpu.VMEM((64, LANES), jnp.float32)]
+    scratch = [pltpu.VMEM((5, 32, LANES), jnp.float32), pltpu.VMEM((5, 8, LANES), jnp.float32)]
     field = shape(COUNT, 8, LANES)
 
     inner, send = call(
@@ -390,7 +469,14 @@
         "ssvvvv",
         [field, shape(8, ROWS0, LANES)],
         scratch,
-        (pos, refined[0], coarse_state[0], fine_state[0], as_matrix(fine_place), as_matrix(coarse_place)),
+        (
+            pos,
+            refined[0],
+            jnp.swapaxes(coarse_state, 0, 1),
+            jnp.swapaxes(fine_state[0], 0, 1),
+            as_matrix(fine_place),
+            as_matrix(coarse_place),
+        ),
     )
     got = swap(send, 0)
     outer, send = call(forward_y, "svv", [field, shape(8, ROWS1, LANES)], [], (pos, got, inner))
@@ -402,11 +488,11 @@
     coarse_out, fine_out = call(
         advance,
         "svvvvv",
-        [shape(5, 512), shape(8, 5, 512)],
+        [shape(5, 1, 512), shape(5, 8, 512)],
         scratch,
         (pos, got, inner, outer, as_matrix(fine_place.T), as_matrix(coarse_place.T)),
     )
-    return coarse_out[None], fine_out[None]
+    return jnp.swapaxes(coarse_out, 0, 1), jnp.swapaxes(fine_out, 0, 1)[None]
 
 
 def solution(mesh):

time: 84.4 us -> 73 us (0.86)
  blocking collectives: 74.8 us -> 64 us
  local copies, waits for them, and re-layouts: 3.75 us -> 2.53 us
    all_to_all x3, blocking collectives: 74.8 us -> 64 us  [swap(): lax.all_to_all(block, 'boxes', 0, 0, axis_index_groups=lines(lax.axis_siz...]
    unnamed x14, local copies, waits for them, and re-layouts: 3.66 us -> 2.45 us
where the time goes in v1:
time: 73 us; the launch traced here: 72.7 us
  blocking collectives  64 us (88%)
  Pallas kernels  5.4 us (7%)
  local copies, waits for them, and re-layouts  2.53 us (3%)
    all_to_all x3, blocking collectives, swap(): lax.all_to_all(block, 'boxes', 0, 0, axis_index_groups=lines(lax.axis_siz...  64 us
    pallas_call x4, Pallas kernels, call(): pl.pallas_call(kernel, out_shape=outs, in_specs=[pl.BlockSpec(memory_spac...  5.4 us
    unnamed x14, local copies, waits for them, and re-layouts  2.45 us

profile of v1, /device:TPU:32, one launch (start us, length us, event | category | flops | bytes accessed | tf_op | source)
XLA Modules:
  0.0 72.7 jit_solution(8303094804082424404)
XLA Ops:
  0.6 0.0 copy-start.4
  0.6 0.0 copy-start.2
  0.7 0.1 stack.27.pos_ref
  0.8 0.0 copy-start.6
  0.8 0.6 copy-done.4
  1.4 0.1 copy-done.2
  1.5 0.0 copy-done.6
  1.5 0.0 copy-start.1
  1.5 0.9 %copy-done.1 = bf16[256,512]{1,0:T(8,128)(2,1)S(1)} copy-done((bf16[256,512]{1,0:T(8,128)(2,1)S(1)}, bf16[256,512]{1,0:T(8,128)(2,1)}, u32[]{:S(2)}) %copy-start.1) | copy-done | bytes 262168
  2.5 0.0 copy-start.5
  2.5 0.7 copy-done.5
  3.2 1.0 %shard_map.86 = (f32[51,8,128]{2,1,0:T(8,128)S(1)}, f32[8,40,128]{2,1,0:T(8,128)S(1)}) custom-call(s32[6]{0:T(128)S(1)} %stack.27.pos_ref, s32[8]{0:T(128)S(1)} %bitcast.17, f32[5,1,512]{2,1,0:T(1,128)S(1)} %bitcast.16, f32[5,8,512]{2,1,0:T(8,128)S(1)} %bitcast.15, bf16[256,512]{1,0:T(8,128)(2,1)S(1)} %copy-done.1, bf16[128,128]{1,0:T(8,128)(2,1)S(1)} %copy-done.4), custom_call_target="tpu_custom_call" | custom-call | tf_op jit(solution)/shard_map/pallas_call | solution.py:432
  4.2 11.6 %all_to_all.15.got_ref = f32[8,40,128]{2,1,0:T(8,128)S(1)} all-to-all(f32[8,40,128]{2,1,0:T(8,128)S(1)} %get-tuple-element.11), channel_id=1, replica_groups={{0,1,8,9,64,65,72,73},{2,3,10,11,66,67,74,75},{4,5,12,13,68,69,76,77},{..., dimensions={0} | all-to-all | bytes 327680 | tf_op jit(solution)/shard_map/all_to_all | solution.py:452
  15.9 0.8 %shard_map.87 = (f32[51,8,128]{2,1,0:T(8,128)S(1)}, f32[8,32,128]{2,1,0:T(8,128)S(1)}) custom-call(s32[6]{0:T(128)S(1)} %stack.27.pos_ref, f32[8,40,128]{2,1,0:T(8,128)S(1)} %all_to_all.15.got_ref, f32[51,8,128]{2,1,0:T(8,128)S(1)} %get-tuple-element.12.inner_ref), custom_call_target="tpu_custom_call" | custom-call | tf_op jit(solution)/shard_map/pallas_call | solution.py:432
  16.6 23.5 %all_to_all.16.got_ref = f32[8,32,128]{2,1,0:T(8,128)S(1)} all-to-all(f32[8,32,128]{2,1,0:T(8,128)S(1)} %get-tuple-element.13), channel_id=1, replica_groups={{0,2,16,18,128,130,144,146},{1,3,17,19,129,131,145,147},{4,6,20,22,132,..., dimensions={0} | all-to-all | bytes 262144 | tf_op jit(solution)/shard_map/all_to_all | solution.py:452
  40.1 0.0 copy-start.3
  40.1 1.0 %shard_map.88 = (f32[51,8,128]{2,1,0:T(8,128)S(1)}, f32[51,8,128]{2,1,0:T(8,128)S(1)}, f32[8,32,128]{2,1,0:T(8,128)S(1)}) custom-call(s32[6]{0:T(128)S(1)} %stack.27.pos_ref, f32[8,32,128]{2,1,0:T(8,128)S(1)} %all_to_all.16.got_ref, f32[51,8,128]{2,1,0:T(8,128)S(1)} %get-tuple-element.12.inner_ref, f32[51,8,128]{2,1,0:T(8,128)S(1)} %get-tuple-element.14.outer_ref), custom_call_target="tpu_custom_call" | custom-call | tf_op jit(solution)/shard_map/pallas_call | solution.py:432
  41.1 0.0 copy-start
  41.1 28.9 %all_to_all.17.got_ref = f32[8,32,128]{2,1,0:T(8,128)S(1)} all-to-all(f32[8,32,128]{2,1,0:T(8,128)S(1)} %get-tuple-element.15), channel_id=1, replica_groups={{0,4,32,36,256,260,288,292},{1,5,33,37,257,261,289,293},{2,6,34,38,258,..., dimensions={0} | all-to-all | bytes 262144 | tf_op jit(solution)/shard_map/all_to_all | solution.py:452
  70.0 0.0 copy-done.3
  70.0 0.0 copy-done
  70.0 2.6 %shard_map.89 = (f32[5,1,512]{2,1,0:T(1,128)}, f32[5,8,512]{2,1,0:T(8,128)}) custom-call(s32[6]{0:T(128)S(1)} %stack.27.pos_ref, f32[8,32,128]{2,1,0:T(8,128)S(1)} %all_to_all.17.got_ref, f32[51,8,128]{2,1,0:T(8,128)S(1)} %get-tuple-element.16.inner_ref, f32[51,8,128]{2,1,0:T(8,128)S(1)} %get-tuple-element.17.outer_ref, bf16[512,256]{1,0:T(8,128)(2,1)S(1)} %copy-done, ...), custom_call_target="tpu_custom_call" | custom-call | tf_op jit(solution)/shard_map/pallas_call | solution.py:432
Async XLA Ops:
  0.6 0.8 %copy-start.4 = (bf16[128,128]{1,0:T(8,128)(2,1)S(1)}, bf16[128,128]{1,0:T(8,128)(2,1)}, u32[]{:S(2)}) copy-start(bf16[128,128]{1,0:T(8,128)(2,1)} %constant.31.clone.place_coarse_ref) | copy-start | bytes 98308
  0.6 0.9 %copy-start.2 = (f32[1,8,5,512]{3,1,2,0:T(8,128)S(1)}, f32[1,8,5,512]{3,1,2,0:T(8,128)}, u32[]{:S(2)}) copy-start(f32[1,8,5,512]{3,1,2,0:T(8,128)} %param.8) | copy-start | bytes 245764
  0.8 0.8 %copy-start.6 = (s32[1,8]{1,0:T(1,128)S(1)}, s32[1,8]{1,0:T(1,128)}, u32[]{:S(2)}) copy-start(s32[1,8]{1,0:T(1,128)} %param.9) | copy-start | bytes 100
  1.5 1.0 %copy-start.1 = (bf16[256,512]{1,0:T(8,128)(2,1)S(1)}, bf16[256,512]{1,0:T(8,128)(2,1)}, u32[]{:S(2)}) copy-start(bf16[256,512]{1,0:T(8,128)(2,1)} %constant.30.clone.place_ref) | copy-start | bytes 786436
  2.5 0.7 copy-start.5
  40.1 29.9 %copy-start.3 = (bf16[128,128]{1,0:T(8,128)(2,1)S(1)}, bf16[128,128]{1,0:T(8,128)(2,1)}, u32[]{:S(2)}) copy-start(bf16[128,128]{1,0:T(8,128)(2,1)} %constant.33.clone.back_coarse_ref) | copy-start | bytes 98308
  41.1 28.9 %copy-start = (bf16[512,256]{1,0:T(8,128)(2,1)S(1)}, bf16[512,256]{1,0:T(8,128)(2,1)}, u32[]{:S(2)}) copy-start(bf16[512,256]{1,0:T(8,128)(2,1)} %constant.32.clone.back_ref) | copy-start | bytes 786436

commit v2 on v1

v2 whole, which is shorter than its diff:
```python
import functools

import jax
import jax.numpy as jnp
import ml_dtypes
import numpy as np
from jax import lax
from jax.experimental import pallas as pl
from jax.experimental.pallas import tpu as pltpu
from jax.sharding import PartitionSpec as P

PITCH = 10
LANES = 128
FINE = 40
COARSE = FINE
DEEP = COARSE + 5
COVER = DEEP + 5
COUNT = COVER + 1
FACE = 28
ROWS = 32
MAX_LANE = 120
PAIRED = 26
SIDES = ((0, 8), (1, -1))
PAIRS = ((0, 1), (0, 2), (1, 2))
gamma_gas = 1.4
courant = 0.4


def placement():
    fine = np.zeros((256, 512), np.float32)
    coarse = np.zeros((128, 128), np.float32)
    for oy in range(2):
        for oz in range(2):
            for j in range(8):
                for k in range(8):
                    row = oy * 128 + oz * 64 + j * 8 + k
                    lane = (oy * 4 + j // 2) * PITCH + oz * 4 + k // 2
                    fine[row, (j % 2 * 2 + k % 2) * 128 + lane] = 1
    for j in range(8):
        for k in range(8):
            coarse[j * 8 + k, j * PITCH + k] = 1
    return fine, coarse


def place(values, matrix):
    high = values.astype(jnp.bfloat16)
    rest = values - high.astype(jnp.float32)
    middle = rest.astype(jnp.bfloat16)
    low = (rest - middle.astype(jnp.float32)).astype(jnp.bfloat16)
    rows = values.shape[0]
    parts = jnp.concatenate([high, middle, low], axis=0)
    out = jnp.dot(parts, matrix, preferred_element_type=jnp.float32)
    return out[:rows] + out[rows : 2 * rows] + out[2 * rows :]


def roll(x, shift, axis):
    shift = shift % x.shape[axis]
    return pltpu.roll(x, shift, axis) if shift else x


def positions(rows):
    row = lax.broadcasted_iota(jnp.int32, (rows, LANES), 0)
    lane = lax.broadcasted_iota(jnp.int32, (rows, LANES), 1)
    x = jnp.where(row > 8, row - 16, row)
    along = (lane + PITCH + 1) & (LANES - 1)
    y1 = (along * 205) >> 11
    return lane, x, y1 - 1, along - y1 * PITCH - 1


def inside(pos):
    return (pos >= 0) & (pos < 8)


def primitive(u):
    inverse = 1.0 / u[0]
    v = [u[1 + d] * inverse for d in range(3)]
    pressure = 0.4 * (u[4] - 0.5 * (u[1] * v[0] + u[2] * v[1] + u[3] * v[2]))
    sound = jnp.sqrt(gamma_gas * pressure * inverse)
    return v, pressure, sound


def cell_flux(u, prim, d):
    v, pressure, sound = prim
    flux = [u[1 + d]] + [u[1 + e] * v[d] for e in range(3)] + [(u[4] + pressure) * v[d]]
    flux[1 + d] = flux[1 + d] + pressure
    return list(u) + flux + [jnp.abs(v[d]) + sound]


def face(left, right):
    speed = jnp.maximum(left[10], right[10])
    return [(left[5 + f] + right[5 + f]) - speed * (right[f] - left[f]) for f in range(5)]


def ahead(x, d):
    return roll(x, -1, 0) if d == 0 else roll(x, -PITCH if d == 1 else -1, 1)


def behind(x, d):
    return roll(x, 1, 0) if d == 0 else roll(x, PITCH if d == 1 else 1, 1)


def fine_net(u, inner):
    prims = [primitive(u[q]) for q in range(8)]
    total = [None] * 8
    for d in range(3):
        bit = 4 >> d
        cut = (lambda x: x[:8]) if inner and d > 0 else (lambda x: x)
        keep = (lambda x: x[:8]) if inner else (lambda x: x)
        for low in range(8):
            if low & bit:
                continue
            high = low | bit
            cells = []
            for q in (low, high):
                v, pressure, sound = prims[q]
                cells.append(cell_flux([cut(x) for x in u[q]], ([cut(x) for x in v], cut(pressure), cut(sound)), d))
            middle = face(cells[0], cells[1])
            after = face(cells[1], [ahead(x, d) for x in cells[0]])
            net_low = [keep(middle[f] - behind(after[f], d)) for f in range(5)]
            net_high = [keep(after[f] - middle[f]) for f in range(5)]
            for q, net in ((low, net_low), (high, net_high)):
                total[q] = net if total[q] is None else [s + n for s, n in zip(total[q], net)]
    return total


def coarse_net(u, deep, pos):
    prim = primitive(u)
    prim_deep = None if deep is None else primitive(deep)
    total = None
    for d in range(3):
        cell = cell_flux(u, prim, d)
        right = [ahead(x, d) for x in cell]
        if deep is not None:
            outer = cell_flux(deep, prim_deep, d)
            last, first = pos[d] == 8, pos[d] == -1
            right = [jnp.where(last, o, r) for o, r in zip(outer, right)]
        after = face(cell, right)
        before = [behind(x, d) for x in after]
        if deep is not None:
            before = [jnp.where(first, o, b) for o, b in zip(face(outer, cell), before)]
        net = [a - b for a, b in zip(after, before)]
        total = net if total is None else [s + n for s, n in zip(total, net)]
    return total


def is_deep(n):
    return DEEP <= n < COVER


def fine_index(f, a, b, c):
    return f * 8 + a * 4 + b * 2 + c


def y_order(near):
    rest = [fine_index(f, a, 1 - near, c) for f in range(5) for a in range(2) for c in range(2)]
    first = [fine_index(f, 1, near, c) for c in range(2) for f in range(5)]
    second = [fine_index(f, 0, near, c) for c in range(2) for f in range(5)]
    return (
        first + [COARSE + f for f in range(5)] + rest[:1],
        second + [DEEP + f for f in range(5)] + [COVER],
        rest[1:17],
        rest[17:],
    )


def z_order(near):
    rest = [fine_index(f, a, b, 1 - near) for f in range(5) for a in range(2) for b in range(2)]
    first = [fine_index(f, 1, b, near) for b in range(2) for f in range(5)]
    second = [fine_index(f, 0, b, near) for b in range(2) for f in range(5)]
    return (
        (first, [COARSE + f for f in range(5)]),
        (second, [DEEP + f for f in range(5)]),
        (rest[:10], [COVER] + rest[10:14]),
        (rest[14:19], rest[19:]),
    )


def block_transpose(value):
    row = lax.broadcasted_iota(jnp.int32, (8, LANES), 0)
    group = lax.broadcasted_iota(jnp.int32, (8, LANES), 1) >> 4
    out = value
    for step in range(1, 8):
        moved = roll(roll(value, -16 * step, 1), step, 0)
        out = jnp.where(((row - group) & 7) == step, moved, out)
    return out


def swapped(flag, first, second):
    return jnp.where(flag, second, first), jnp.where(flag, first, second)


def prepare(
    pos_ref, refined_ref, coarse_ref, fine_ref, place_ref, place_coarse_ref, dense_ref, inner_ref, send_ref, scr, scr_c, scr_x
):
    lane, x, y, z = positions(8)
    row = lax.broadcasted_iota(jnp.int32, (8, LANES), 0)
    left_half = lane < 64
    for f in range(5):
        for q in range(4):
            tile = fine_ref[f, :, q * 128 : q * 128 + 128]
            for ox in range(2):
                scr[f, pl.ds(ox * 4 + q, 4, stride=8), :] = tile[ox * 4 : ox * 4 + 4]
            part = coarse_ref[f, :, q * 128 : q * 128 + 128]
            scr_c[f, 2 * q : 2 * q + 1, :] = part
            scr_c[f, 2 * q + 1 : 2 * q + 2, :] = part
    sides = [[], []]
    rows = []
    for f in range(5):
        tile = [scr[f, c * 8 : c * 8 + 8, :] for c in range(4)]
        sides[0].append(
            jnp.concatenate([jnp.where(left_half, tile[2 * h], roll(tile[2 * h + 1], 64, 1)) for h in range(2)], axis=1)
        )
        sides[1].append(
            jnp.concatenate([jnp.where(left_half, roll(tile[2 * h], 64, 1), tile[2 * h + 1]) for h in range(2)], axis=1)
        )
        value = scr_c[f]
        rows.append(jnp.where((row & 1) == 1, roll(value, 64, 1), value))
    fine = place(jnp.concatenate(sides[0] + sides[1], axis=0), place_ref[...])
    coarse = place(jnp.concatenate(rows, axis=0), place_coarse_ref[...])
    coarse = [coarse[f * 8 : f * 8 + 8] for f in range(5)]

    covered = jnp.zeros((8, LANES), jnp.float32)
    for o in range(8):
        here = ((x >= 4) == (o >= 4)) & ((y >= 4) == (o % 4 >= 2)) & ((z >= 4) == (o % 2 == 1))
        covered = jnp.where(here, (refined_ref[o] > 0).astype(jnp.float32), covered)
    state = []
    for f in range(5):
        for q in range(8):
            first = (q // 4 * 5 + f) * 8
            part = fine[first : first + 8, q % 4 * 128 : q % 4 * 128 + 128]
            state.append(jnp.where(covered > 0.5, part, coarse[f]))
    state += coarse
    fastest = None
    for u in [[state[f * 8 + q] for f in range(5)] for q in range(8)] + [coarse]:
        v, pressure, sound = primitive(u)
        speed = jnp.abs(v[0]) + jnp.abs(v[1]) + jnp.abs(v[2]) + 3.0 * sound
        fastest = speed if fastest is None else jnp.maximum(fastest, speed)
    fastest = jnp.where(inside(y) & inside(z), fastest, 0.0)
    fastest = jnp.broadcast_to(jnp.max(fastest), (8, LANES))

    zero = jnp.zeros((8, LANES), jnp.float32)
    stored = state + [zero] * 5 + [covered]
    for n in range(COUNT):
        inner_ref[n] = stored[n]

    own = pos_ref[0]
    far = [pos_ref[3 + d] for d in range(3)]
    for t in range(8):
        send_ref[t, 0, FACE - 1 : FACE, :] = fastest[:1]

    def taken(n, at, deep_at):
        return (stored[n - 5], deep_at) if is_deep(n) else (stored[n], at)

    for side, at, deep_at in ((0, 7, 6), (1, 0, 1)):
        for n in range(COUNT):
            value, where = taken(n, at, deep_at)
            target = side * 64 + (n if n < PAIRED else n - PAIRED + 32)
            scr_x[target : target + 1, :] = value[where : where + 1, :]
    dense = place(scr_x[...], dense_ref[...])
    left4 = lax.broadcasted_iota(jnp.int32, (32, LANES), 1) < 64
    row32 = lax.broadcasted_iota(jnp.int32, (32, LANES), 0)
    for side in range(2):
        packed = jnp.where(left4, dense[side * 64 : side * 64 + 32], roll(dense[side * 64 + 32 : side * 64 + 64], 64, 1))
        packed = jnp.where(row32 >= PAIRED, jnp.concatenate([fastest] * 4, axis=0), packed)
        send_ref[own ^ 1, far[0] if side == 0 else 1 - far[0]] = packed

    slots = lane - ((lane * 205) >> 11) * PITCH
    corners_xy, corners_xz, corners = [], [], zero
    for side, at, deep_at in ((0, 7, 6), (1, 0, 1)):
        near = 1 - side
        order = y_order(near)
        blocks = []
        for names in order:
            packed = fastest
            for s, n in enumerate(names):
                value, where = taken(n, at, deep_at)
                packed = jnp.where((lane >> 3) == s, roll(value, s * 8 - where * PITCH, 1), packed)
            blocks.append(packed)
        width = len(order[3]) * 8
        second = (lane >= width) & (lane < 2 * width)
        blocks[3] = jnp.where(second, roll(roll(blocks[3], width, 1), 4, 0), blocks[3])
        part = far[1] if side == 0 else 1 - far[1]
        for block in range(3):
            send_ref[own ^ 2, part, block * 8 : block * 8 + 8, :] = blocks[block]
        send_ref[own ^ 2, part, 24:FACE, :] = blocks[3][:4]
        corners_xy.append((blocks[0][7:8], jnp.where(lane < 80, blocks[1], blocks[0])[0:1]))

        blocks = []
        for block, (names, halves) in enumerate(z_order(near)):
            packed = fastest
            for s, n in enumerate(names):
                value, where = taken(n, at, deep_at)
                packed = jnp.where((slots == s) & (lane < 80), roll(value, s - where, 1), packed)
            if block < 3:
                extra = fastest
                for s, n in enumerate(halves):
                    value, where = taken(n, at, deep_at)
                    extra = jnp.where(slots == s, roll(value, s - where, 1), extra)
                extra = jnp.where(slots < 5, roll(extra, 80, 1), roll(extra, 45, 1))
                packed = jnp.where((lane >= 80) & (lane < MAX_LANE), extra, packed)
            else:
                second = (slots >= 5) & (lane < 80)
                packed = jnp.where(second, roll(roll(packed, 5, 1), 4, 0), packed)
                value = stored[halves[0]]
                lower = roll(value, 4, 0)
                pieces = [roll(value, 80 - at, 1), roll(value, 41 - at, 1), roll(lower, 82 - at, 1), roll(lower, 43 - at, 1)]
                for s, piece in enumerate(pieces):
                    packed = jnp.where((slots == s) & (lane >= 80) & (lane < MAX_LANE), piece, packed)
            blocks.append(packed)
        part = far[2] if side == 0 else 1 - far[2]
        for block in range(3):
            send_ref[own ^ 4, part, block * 8 : block * 8 + 8, :] = blocks[block]
        send_ref[own ^ 4, part, 24:FACE, :] = blocks[3][:4]
        corners_xz.append((blocks[0][7:8], jnp.where(lane < 80, blocks[1], blocks[0])[0:1]))
        for end, first, first_coarse in ((0, 75, 115), (1, 0, 80)):
            to = (side * 2 + end) * 16
            for start, source, i in ((first, blocks[0], 0), (first, blocks[1], 5), (first_coarse, blocks[0], 10)):
                here = (lane >= to + i) & (lane < to + i + 5)
                corners = jnp.where(here, roll(source, to + i - start, 1), corners)
    corners = block_transpose(corners)

    edges = [
        [[corners_xy[e][d] for e in range(2)] for d in range(2)],
        [[corners_xz[e][d] for e in range(2)] for d in range(2)],
        [[corners[e * 2 + d : e * 2 + d + 1] for e in range(2)] for d in range(2)],
    ]
    for (d, e), edge in zip(PAIRS, edges):
        upper, lower = [swapped(far[e] == 1, *half) for half in edge]
        near_near, far_near = swapped(far[d] == 1, upper[0], lower[0])
        near_far, far_far = swapped(far[d] == 1, upper[1], lower[1])
        for r, value in enumerate((near_near, near_far, far_near, far_far)):
            send_ref[own ^ (1 << d) ^ (1 << e), 0, r : r + 1, :] = value


def others(d):
    return [e for e in range(3) if e != d]


def pair(d, e):
    return (1 << d) ^ (1 << e)


def running_maximum(rows):
    fastest = functools.reduce(jnp.maximum, rows)
    lane = lax.broadcasted_iota(jnp.int32, fastest.shape, 1)
    fastest = jnp.where(lane >= MAX_LANE, fastest, 0.0)
    return jnp.broadcast_to(jnp.max(fastest), (1, LANES))


def pass_on(send_ref, own, fastest, faces, edges, corners):
    lane = lax.broadcasted_iota(jnp.int32, (1, LANES), 1)
    for t in range(8):
        send_ref[t, FACE - 1 : FACE, :] = fastest
    for d in range(3):
        slot = own ^ (1 << d)
        send_ref[slot, : FACE - 1, :] = faces[d](0, FACE - 1)
        last = faces[d](FACE - 1, FACE)
        send_ref[slot, FACE - 1 : FACE, :] = jnp.where(lane >= MAX_LANE, fastest, last)
        for r, value in enumerate(edges[d]):
            send_ref[slot, FACE + r : FACE + r + 1, :] = value
    for (d, e), value in zip(PAIRS, corners):
        send_ref[own ^ pair(d, e), 0:1, :] = value


def carry_once(pos_ref, got_ref, send_ref):
    own, to = pos_ref[0], pos_ref[1]
    fastest = running_maximum([got_ref[t, 0, FACE - 1 : FACE, :] for t in range(8)])
    faces = [lambda i, j, d=d: got_ref[own ^ (1 << d), 1, i:j, :] for d in range(3)]

    def edge(d, e, r):
        return got_ref[own ^ pair(d, e), 0, r : r + 1, :]

    edges = [[edge(d, e, 1 if e < d else 2) for e in others(d)] for d in range(3)]
    pass_on(send_ref, to, fastest, faces, edges, [edge(d, e, 3) for d, e in PAIRS])


def carry_twice(pos_ref, got_ref, send_ref):
    own, to = pos_ref[1], pos_ref[2]
    fastest = running_maximum([got_ref[t, FACE - 1 : FACE, :] for t in range(8)])
    faces = [lambda i, j, d=d: got_ref[own ^ (1 << d), i:j, :] for d in range(3)]

    def far_far(d, e):
        return got_ref[own ^ pair(d, e), 0:1, :]

    edges = []
    for d in range(3):
        passed = [got_ref[own ^ (1 << d), FACE + r : FACE + r + 1, :] for r in range(2)]
        edges.append(passed + [far_far(d, e) for e in others(d)])
    pass_on(send_ref, to, fastest, faces, edges, [far_far(d, e) for d, e in PAIRS])


def arrived(pos_ref, got0, got1, got2):
    own = [pos_ref[i] for i in range(3)]
    upper_far = [pos_ref[3 + d] == 1 for d in range(3)]
    twice = [pos_ref[6 + d] == 1 for d in range(3)]
    faces = []
    for d in range(3):
        near = got0[own[0] ^ (1 << d), 0]
        far = jnp.where(twice[d], got2[own[2] ^ (1 << d)], got1[own[1] ^ (1 << d)])
        faces.append(swapped(upper_far[d], near, far))

    def once(d, r):
        return got1[own[1] ^ (1 << d), FACE + r : FACE + r + 1, :]

    def again(d, r):
        return got2[own[2] ^ (1 << d), FACE + r : FACE + r + 1, :]

    edges = []
    for d, e in PAIRS:
        of_e, of_d = others(d).index(e), others(e).index(d)
        near_near = got0[own[0] ^ pair(d, e), 0, 0:1, :]
        near_far = jnp.where(twice[e], again(e, of_d), once(e, of_d))
        far_near = jnp.where(twice[d], again(d, of_e), once(d, of_e))
        both = jnp.where(twice[e], got2[own[2] ^ pair(d, e), 0:1, :], again(d, 2 + of_e))
        neither = jnp.where(twice[e], again(e, 2 + of_d), got1[own[1] ^ pair(d, e), 0:1, :])
        far_far = jnp.where(twice[d], both, neither)
        near, far = [swapped(upper_far[e], *half) for half in ((near_near, near_far), (far_near, far_far))]
        above, below = zip(*[swapped(upper_far[d], n, f) for n, f in zip(near, far)])
        edges.append((above, below))
    return faces, edges


def surround(faces, edges, inner_ref, spread_ref, scr_x):
    lane, x, y, z = positions(8)
    row = lax.broadcasted_iota(jnp.int32, (8, LANES), 0)
    left4 = lax.broadcasted_iota(jnp.int32, (32, LANES), 1) < 64
    inner = [inner_ref[n] for n in range(COUNT)]
    rows = []
    for side in range(2):
        value = faces[0][side]
        rows += [jnp.where(left4, value, 0.0), jnp.where(left4, roll(value, 64, 1), 0.0)]
    scr_x[...] = place(jnp.concatenate(rows, axis=0), spread_ref[...])
    outer = []
    for n in range(COUNT):
        at = n if n < PAIRED else n - PAIRED + 32
        above = jnp.broadcast_to(scr_x[at : at + 1, :], (8, LANES))
        below = jnp.broadcast_to(scr_x[at + 64 : at + 65, :], (8, LANES))
        outer.append(jnp.where(row == 0, above, below))

    def doubled(value):
        return jnp.concatenate([value[24:28], value[24:28]], axis=0)

    for side, (near, at) in enumerate(SIDES):
        blocks = [faces[1][side][block * 8 : block * 8 + 8] for block in range(3)]
        order = y_order(near)
        first = at * PITCH % LANES
        here = (lane >= first) & (lane < first + 8)
        for block, names in zip(blocks, order):
            for s, n in enumerate(names):
                inner[n] = jnp.where(here, roll(block, first - s * 8, 1), inner[n])
        last = doubled(faces[1][side])
        for s, n in enumerate(order[3]):
            value = jnp.where(row < 4, roll(last, first - s * 8, 1), roll(last, first - (s + len(order[3])) * 8, 1))
            inner[n] = jnp.where(here, value, inner[n])
        above, below = [jnp.broadcast_to(edges[0][end][side], (8, LANES)) for end in range(2)]
        edge = jnp.where(row == 0, above, below)
        for s in range(15):
            value = roll(edge, first - s * 8, 1)
            for n in (order[0][s], order[1][s]) if s < 10 else (order[0][s],):
                outer[n] = jnp.where(here, value, outer[n])

    columns = jnp.concatenate([edges[2][end][side] for side in range(2) for end in range(2)] * 2, axis=0)
    columns = block_transpose(columns)
    for side, (near, at) in enumerate(SIDES):
        blocks = [faces[2][side][block * 8 : block * 8 + 8] for block in range(3)]
        order = z_order(near)
        here = (z == at) & (y < 9)
        low_y = y < 4
        above, below = side * 32, side * 32 + 16

        def joined(block):
            return jnp.where(lane < 40, roll(block, -80, 1), roll(block, -45, 1))

        def ended(block, i, below_lane):
            block = jnp.where(lane < 80, block, roll(columns, 80 - above - i, 1))
            return jnp.where(lane >= below_lane, roll(columns, below_lane - below - i, 1), block)

        mains = [ended(blocks[0], 0, 123), ended(blocks[1], 5, 123), blocks[2]]
        halves = [ended(joined(blocks[0]), 10, 118), joined(blocks[1]), joined(blocks[2])]
        for block in range(3):
            for source, names in ((mains[block], order[block][0]), (halves[block], order[block][1])):
                for s, n in enumerate(names):
                    inner[n] = jnp.where(here, roll(source, at - s, 1), inner[n])
        last = doubled(faces[2][side])
        for s, n in enumerate(order[3][0]):
            value = jnp.where(row < 4, roll(last, at - s, 1), roll(last, at - 5 - s, 1))
            inner[n] = jnp.where(here, value, inner[n])
        upper_rows = jnp.where(low_y, roll(last, at - 80, 1), roll(last, at - 41, 1))
        lower_rows = jnp.where(low_y, roll(last, at - 82, 1), roll(last, at - 43, 1))
        n = order[3][1][0]
        inner[n] = jnp.where(here, jnp.where(row < 4, upper_rows, lower_rows), inner[n])

        above, below = [jnp.broadcast_to(edges[1][end][side], (8, LANES)) for end in range(2)]
        edge = jnp.where(row == 0, above, below)
        for s in range(10):
            value = roll(edge, at - s, 1)
            for n in (order[0][0][s], order[1][0][s]):
                outer[n] = jnp.where(here & inside(y), value, outer[n])
        edge = joined(edge)
        for s in range(5):
            n = COARSE + s
            outer[n] = jnp.where(here & inside(y), roll(edge, at - s, 1), outer[n])
    return [jnp.concatenate([i, o], axis=0) for i, o in zip(inner, outer)]


def advance(
    pos_ref, got0, got1, got2, inner_ref, spread_ref, back_ref, back_coarse_ref, coarse_out, fine_out, scr, scr_x
):
    lane, x, y, z = positions(16)
    fastest = running_maximum([got2[t, FACE - 1 : FACE, :] for t in range(8)])
    half16 = 0.5 * (courant / jnp.broadcast_to(fastest, (16, LANES)))
    half = half16[:8]
    faces, edges = arrived(pos_ref, got0, got1, got2)
    state = surround(faces, edges, inner_ref, spread_ref, scr_x)
    covered = state[COVER] > 0.5
    fine0 = [[state[f * 8 + q] for f in range(5)] for q in range(8)]
    coarse0 = state[COARSE:DEEP]

    net = coarse_net(coarse0, state[DEEP:COVER], (x, y, z))
    coarse1 = [u - 0.5 * half16 * n for u, n in zip(coarse0, net)]
    net = fine_net(fine0, False)
    fine1 = [
        [jnp.where(covered, fine0[q][f] - half16 * net[q][f], coarse1[f]) for f in range(5)] for q in range(8)
    ]
    net = coarse_net(coarse1, None, None)
    coarse2 = [0.5 * c0[:8] + 0.5 * (c1[:8] - 0.5 * half * n[:8]) for c0, c1, n in zip(coarse0, coarse1, net)]
    net = fine_net(fine1, True)
    mine = inside(y[:8]) & inside(z[:8])
    refined = mine & covered[:8]
    fine2 = [
        [
            jnp.where(refined, 0.5 * fine0[q][f][:8] + 0.5 * (fine1[q][f][:8] - half * net[q][f]), 0.0)
            for f in range(5)
        ]
        for q in range(8)
    ]
    coarse = []
    for f in range(5):
        total = functools.reduce(jnp.add, [fine2[q][f] for q in range(8)])
        coarse.append(jnp.where(mine, jnp.where(refined, 0.125 * total, coarse2[f]), 0.0))

    left_half = lane[:8] < 64
    rows = [jnp.concatenate([fine2[a * 4 + q][f] for q in range(4)], axis=1) for a in range(2) for f in range(5)]
    back = place(jnp.concatenate(rows, axis=0), back_ref[...])
    for f in range(5):
        for h in range(2):
            even = back[f * 8 : f * 8 + 8, h * 128 : h * 128 + 128]
            odd = back[40 + f * 8 : 48 + f * 8, h * 128 : h * 128 + 128]
            scr[f, h * 16 : h * 16 + 8, :] = jnp.where(left_half, even, roll(odd, 64, 1))
            scr[f, h * 16 + 8 : h * 16 + 16, :] = jnp.where(left_half, roll(even, 64, 1), odd)
        for q in range(4):
            for ox in range(2):
                tile = scr[f, pl.ds(ox * 4 + q, 4, stride=8), :]
                fine_out[f, ox * 4 : ox * 4 + 4, q * 128 : q * 128 + 128] = tile
    back = place(jnp.concatenate(coarse, axis=0), back_coarse_ref[...])
    for f in range(5):
        value = back[f * 8 : f * 8 + 8]
        value = jnp.where(left_half, value, roll(roll(value, 64, 1), -1, 0))
        for q in range(4):
            coarse_out[f, :, q * 128 : q * 128 + 128] = value[2 * q : 2 * q + 1]


def shape(*dims):
    return jax.ShapeDtypeStruct(dims, jnp.float32)


def call(kernel, kinds, outs, scratch, args):
    spaces = {"s": pltpu.SMEM, "v": pltpu.VMEM}
    return pl.pallas_call(
        kernel,
        out_shape=outs,
        in_specs=[pl.BlockSpec(memory_space=spaces[k]) for k in kinds],
        out_specs=[pl.BlockSpec(memory_space=pltpu.VMEM)] * len(outs),
        scratch_shapes=[pltpu.VMEM(dims, jnp.float32) for dims in scratch],
        compiler_params=pltpu.CompilerParams(vmem_limit_bytes=32 * 1024 * 1024),
    )(*args)


def swap(block, level):
    count = lax.axis_size("boxes")
    mask = 7 << (3 * level)
    groups = {}
    for device in range(count):
        groups.setdefault(device & ~mask, []).append(device)
    return lax.all_to_all(block, "boxes", 0, 0, axis_index_groups=list(groups.values()))


def local(coarse_state, fine_state, refined):
    fine_place, coarse_place = placement()
    as_matrix = lambda m: jnp.asarray(np.ascontiguousarray(m).astype(ml_dtypes.bfloat16))
    device = lax.axis_index("boxes")
    levels = [(device >> (3 * level)) & 7 for level in range(3)]
    bits = [[(level >> d) & 1 for d in range(3)] for level in levels]
    twice = [(bits[0][d] == bits[1][d]).astype(jnp.int32) for d in range(3)]
    pos = jnp.stack(levels + bits[0] + twice).astype(jnp.int32)
    spread, dense = as_matrix(coarse_place), as_matrix(coarse_place.T)

    inner, send = call(
        prepare,
        "ssvvvvv",
        [shape(COUNT, 8, LANES), shape(8, 2, ROWS, LANES)],
        [(5, 32, LANES), (5, 8, LANES), (128, LANES)],
        (
            pos,
            refined[0],
            jnp.swapaxes(coarse_state, 0, 1),
            jnp.swapaxes(fine_state[0], 0, 1),
            as_matrix(fine_place),
            spread,
            dense,
        ),
    )
    got0 = swap(send, 0)
    got1 = swap(call(carry_once, "sv", [shape(8, ROWS, LANES)], [], (pos, got0))[0], 1)
    got2 = swap(call(carry_twice, "sv", [shape(8, ROWS, LANES)], [], (pos, got1))[0], 2)
    coarse_out, fine_out = call(
        advance,
        "svvvvvvv",
        [shape(5, 1, 512), shape(5, 8, 512)],
        [(5, 32, LANES), (128, LANES)],
        (pos, got0, got1, got2, inner, spread, as_matrix(fine_place.T), dense),
    )
    return jnp.swapaxes(coarse_out, 0, 1), jnp.swapaxes(fine_out, 0, 1)[None]


def solution(mesh):
    in_specs = (P("boxes", None, None), P("boxes", None, None, None), P("boxes", None))
    out_specs = (P("boxes", None, None), P("boxes", None, None, None))
    return jax.shard_map(local, mesh=mesh, in_specs=in_specs, out_specs=out_specs, check_vma=False)
```

time: 73 us -> 60.5 us (0.83)
  blocking collectives: 64 us -> 51.1 us
    all_to_all x3, blocking collectives: 64 us -> 51.1 us  [swap(): lax.all_to_all(block, 'boxes', 0, 0, axis_index_groups=list(groups.values...]
where the time goes in v2:
time: 60.5 us; the launch traced here: 60.1 us
  blocking collectives  51.1 us (84%)
  Pallas kernels  5.73 us (9%)
  local copies, waits for them, and re-layouts  2.6 us (4%)
  between operations  0.7 us (1%)
    all_to_all x3, blocking collectives, swap(): lax.all_to_all(block, 'boxes', 0, 0, axis_index_groups=list(groups.values...  51.1 us
    pallas_call x4, Pallas kernels, call(): pl.pallas_call(kernel, out_shape=outs, in_specs=[pl.BlockSpec(memory_spac...  5.73 us
    unnamed x14, local copies, waits for them, and re-layouts  2.51 us

profile of v2, /device:TPU:32, one launch (start us, length us, event | category | flops | bytes accessed | tf_op | source)
XLA Modules:
  0.0 60.1 jit_solution(14057329489010411112)
XLA Ops:
  0.6 0.0 copy-start.5
  0.6 0.0 copy-start.3
  0.7 0.0 copy-start.2
  0.7 0.1 stack.51.pos_ref
  0.8 0.0 copy-start.6
  0.8 0.6 copy-done.5
  1.3 0.1 copy-done.3
  1.4 0.0 copy-done.2
  1.4 0.0 copy-done.6
  1.4 0.0 copy-start
  1.4 0.9 %copy-done = bf16[256,512]{1,0:T(8,128)(2,1)S(1)} copy-done((bf16[256,512]{1,0:T(8,128)(2,1)S(1)}, bf16[256,512]{1,0:T(8,128)(2,1)}, u32[]{:S(2)}) %copy-start) | copy-done | bytes 262168
  2.4 0.0 copy-start.4
  2.4 0.9 %copy-done.4 = f32[1,8,5,512]{3,1,2,0:T(8,128)S(1)} copy-done((f32[1,8,5,512]{3,1,2,0:T(8,128)S(1)}, f32[1,8,5,512]{3,1,2,0:T(8,128)}, u32[]{:S(2)}) %copy-start.4) | copy-done | bytes 81944
  3.3 1.3 %shard_map.86 = (f32[51,8,128]{2,1,0:T(8,128)S(1)}, f32[8,2,32,128]{3,2,1,0:T(8,128)S(1)}) custom-call(s32[9]{0:T(128)S(1)} %stack.51.pos_ref, s32[8]{0:T(128)S(1)} %bitcast.20, f32[5,1,512]{2,1,0:T(1,128)S(1)} %bitcast.19, f32[5,8,512]{2,1,0:T(8,128)S(1)} %bitcast.18, bf16[256,512]{1,0:T(8,128)(2,1)S(1)} %copy-done, bf16[128,128]{1,0:T(8,128)(2,1)S(1)} %copy-done.3, ...), custom_call_target="tpu_custom_call" | custom-call | tf_op jit(solution)/shard_map/pallas_call | solution.py:569
  4.6 11.8 %all_to_all.15.got_ref.got0 = f32[8,2,32,128]{3,2,1,0:T(8,128)S(1)} all-to-all(f32[8,2,32,128]{3,2,1,0:T(8,128)S(1)} %get-tuple-element.6), channel_id=1, replica_groups={{0,1,2,3,4,5,6,7},{8,9,10,11,12,13,14,15},{16,17,18,19,20,21,22,23},{24..., dimensions={0} | all-to-all | bytes 524288 | tf_op jit(solution)/shard_map/all_to_all | solution.py:585
  16.4 0.7 %shard_map.87 = f32[8,32,128]{2,1,0:T(8,128)S(1)} custom-call(s32[9]{0:T(128)S(1)} %stack.51.pos_ref, f32[8,2,32,128]{3,2,1,0:T(8,128)S(1)} %all_to_all.15.got_ref.got0), custom_call_target="tpu_custom_call" | custom-call | tf_op jit(solution)/shard_map/pallas_call | solution.py:569
  17.1 11.2 %all_to_all.16.got_ref.got1 = f32[8,32,128]{2,1,0:T(8,128)S(1)} all-to-all(f32[8,32,128]{2,1,0:T(8,128)S(1)} %shard_map.87), channel_id=1, replica_groups={{0,8,16,24,32,40,48,56},{1,9,17,25,33,41,49,57},{2,10,18,26,34,42,50,58..., dimensions={0} | all-to-all | bytes 262144 | tf_op jit(solution)/shard_map/all_to_all | solution.py:585
  28.4 0.0 copy-start.1
  28.4 0.7 %shard_map.88 = f32[8,32,128]{2,1,0:T(8,128)S(1)} custom-call(s32[9]{0:T(128)S(1)} %stack.51.pos_ref, f32[8,32,128]{2,1,0:T(8,128)S(1)} %all_to_all.16.got_ref.got1), custom_call_target="tpu_custom_call" | custom-call | tf_op jit(solution)/shard_map/pallas_call | solution.py:569
  29.0 28.0 %all_to_all.17.got2 = f32[8,32,128]{2,1,0:T(8,128)S(1)} all-to-all(f32[8,32,128]{2,1,0:T(8,128)S(1)} %shard_map.88), channel_id=1, replica_groups={{0,64,128,192,256,320,384,448},{1,65,129,193,257,321,385,449},{2,66,130..., dimensions={0} | all-to-all | bytes 262144 | tf_op jit(solution)/shard_map/all_to_all | solution.py:585
  57.1 0.0 copy-done.1
  57.1 3.0 %shard_map.89 = (f32[5,1,512]{2,1,0:T(1,128)}, f32[5,8,512]{2,1,0:T(8,128)}) custom-call(s32[9]{0:T(128)S(1)} %stack.51.pos_ref, f32[8,2,32,128]{3,2,1,0:T(8,128)S(1)} %all_to_all.15.got_ref.got0, f32[8,32,128]{2,1,0:T(8,128)S(1)} %all_to_all.16.got_ref.got1, f32[8,32,128]{2,1,0:T(8,128)S(1)} %all_to_all.17.got2, ...), custom_call_target="tpu_custom_call" | custom-call | tf_op jit(solution)/shard_map/pallas_call | solution.py:569
Async XLA Ops:
  0.6 0.7 %copy-start.5 = (f32[1,5,512]{2,0,1:T(1,128)S(1)}, f32[1,5,512]{2,0,1:T(1,128)}, u32[]{:S(2)}) copy-start(f32[1,5,512]{2,0,1:T(1,128)} %param.7) | copy-start | bytes 30724
  0.6 0.8 %copy-start.3 = (bf16[128,128]{1,0:T(8,128)(2,1)S(1)}, bf16[128,128]{1,0:T(8,128)(2,1)}, u32[]{:S(2)}) copy-start(bf16[128,128]{1,0:T(8,128)(2,1)} %constant.24.clone.place_coarse_ref.spread_ref) | copy-start | bytes 98308
  0.7 0.8 %copy-start.2 = (bf16[128,128]{1,0:T(8,128)(2,1)S(1)}, bf16[128,128]{1,0:T(8,128)(2,1)}, u32[]{:S(2)}) copy-start(bf16[128,128]{1,0:T(8,128)(2,1)} %constant.25.clone.dense_ref.back_coarse_ref) | copy-start | bytes 98308
  0.8 0.7 %copy-start.6 = (s32[1,8]{1,0:T(1,128)S(1)}, s32[1,8]{1,0:T(1,128)}, u32[]{:S(2)}) copy-start(s32[1,8]{1,0:T(1,128)} %param.9) | copy-start | bytes 100
  1.4 0.9 %copy-start = (bf16[256,512]{1,0:T(8,128)(2,1)S(1)}, bf16[256,512]{1,0:T(8,128)(2,1)}, u32[]{:S(2)}) copy-start(bf16[256,512]{1,0:T(8,128)(2,1)} %constant.26.clone.place_ref) | copy-start | bytes 786436
  2.4 0.9 %copy-start.4 = (f32[1,8,5,512]{3,1,2,0:T(8,128)S(1)}, f32[1,8,5,512]{3,1,2,0:T(8,128)}, u32[]{:S(2)}) copy-start(f32[1,8,5,512]{3,1,2,0:T(8,128)} %param.8) | copy-start | bytes 245764
  28.4 28.7 %copy-start.1 = (bf16[512,256]{1,0:T(8,128)(2,1)S(1)}, bf16[512,256]{1,0:T(8,128)(2,1)}, u32[]{:S(2)}) copy-start(bf16[512,256]{1,0:T(8,128)(2,1)} %constant.27.clone.back_ref) | copy-start | bytes 786436

commit v3 on v2

--- a/solution.py
+++ b/solution.py
@@ -20,6 +20,7 @@
 ROWS = 32
 MAX_LANE = 120
 PAIRED = 26
+LEAD = (1, 4, 4)
 SIDES = ((0, 8), (1, -1))
 PAIRS = ((0, 1), (0, 2), (1, 2))
 gamma_gas = 1.4
@@ -578,11 +579,10 @@
 
 def swap(block, level):
     count = lax.axis_size("boxes")
-    mask = 7 << (3 * level)
-    groups = {}
-    for device in range(count):
-        groups.setdefault(device & ~mask, []).append(device)
-    return lax.all_to_all(block, "boxes", 0, 0, axis_index_groups=list(groups.values()))
+    low = 3 * level
+    first = [device for device in range(count) if not (device >> low) & 7]
+    groups = [[device | (slot ^ LEAD[level]) << low for slot in range(8)] for device in first]
+    return lax.all_to_all(block, "boxes", 0, 0, axis_index_groups=groups)
 
 
 def local(coarse_state, fine_state, refined):
@@ -591,6 +591,7 @@
     device = lax.axis_index("boxes")
     levels = [(device >> (3 * level)) & 7 for level in range(3)]
     bits = [[(level >> d) & 1 for d in range(3)] for level in levels]
+    levels = [level ^ lead for level, lead in zip(levels, LEAD)]
     twice = [(bits[0][d] == bits[1][d]).astype(jnp.int32) for d in range(3)]
     pos = jnp.stack(levels + bits[0] + twice).astype(jnp.int32)
     spread, dense = as_matrix(coarse_place), as_matrix(coarse_place.T)

time: 60.5 us -> 54.4 us (0.90)
  blocking collectives: 51.1 us -> 45 us
    all_to_all x3, blocking collectives: 51.1 us -> 45 us  [swap(): return lax.all_to_all(block, 'boxes', 0, 0, axis_index_groups=groups)]
where the time goes in v3:
time: 54.4 us; the launch traced here: 54 us
  blocking collectives  45 us (83%)
  Pallas kernels  5.73 us (11%)
  local copies, waits for them, and re-layouts  2.6 us (5%)
  between operations  0.7 us (1%)
    all_to_all x3, blocking collectives, swap(): return lax.all_to_all(block, 'boxes', 0, 0, axis_index_groups=groups)  45 us
    pallas_call x4, Pallas kernels, call(): pl.pallas_call(kernel, out_shape=outs, in_specs=[pl.BlockSpec(memory_spac...  5.73 us
    unnamed x14, local copies, waits for them, and re-layouts  2.51 us

profile of v3, /device:TPU:32, one launch (start us, length us, event | category | flops | bytes accessed | tf_op | source)
XLA Modules:
  0.0 54.0 jit_solution(16446532488243216237)
XLA Ops:
  0.6 0.0 copy-start.5
  0.6 0.0 copy-start.3
  0.7 0.0 copy-start.2
  0.7 0.1 stack.51.pos_ref
  0.8 0.0 copy-start.6
  0.8 0.6 %copy-done.5 = f32[1,5,512]{2,0,1:T(1,128)S(1)} copy-done((f32[1,5,512]{2,0,1:T(1,128)S(1)}, f32[1,5,512]{2,0,1:T(1,128)}, u32[]{:S(2)}) %copy-start.5) | copy-done | bytes 10264
  1.3 0.1 copy-done.3
  1.4 0.0 copy-done.2
  1.4 0.0 copy-done.6
  1.4 0.0 copy-start
  1.4 0.9 %copy-done = bf16[256,512]{1,0:T(8,128)(2,1)S(1)} copy-done((bf16[256,512]{1,0:T(8,128)(2,1)S(1)}, bf16[256,512]{1,0:T(8,128)(2,1)}, u32[]{:S(2)}) %copy-start) | copy-done | bytes 262168
  2.4 0.0 copy-start.4
  2.4 0.9 %copy-done.4 = f32[1,8,5,512]{3,1,2,0:T(8,128)S(1)} copy-done((f32[1,8,5,512]{3,1,2,0:T(8,128)S(1)}, f32[1,8,5,512]{3,1,2,0:T(8,128)}, u32[]{:S(2)}) %copy-start.4) | copy-done | bytes 81944
  3.3 1.4 %shard_map.86 = (f32[51,8,128]{2,1,0:T(8,128)S(1)}, f32[8,2,32,128]{3,2,1,0:T(8,128)S(1)}) custom-call(s32[9]{0:T(128)S(1)} %stack.51.pos_ref, s32[8]{0:T(128)S(1)} %bitcast.20, f32[5,1,512]{2,1,0:T(1,128)S(1)} %bitcast.19, f32[5,8,512]{2,1,0:T(8,128)S(1)} %bitcast.18, bf16[256,512]{1,0:T(8,128)(2,1)S(1)} %copy-done, bf16[128,128]{1,0:T(8,128)(2,1)S(1)} %copy-done.3, ...), custom_call_target="tpu_custom_call" | custom-call | tf_op jit(solution)/shard_map/pallas_call | solution.py:570
  4.6 11.5 %all_to_all.15.got_ref.got0 = f32[8,2,32,128]{3,2,1,0:T(8,128)S(1)} all-to-all(f32[8,2,32,128]{3,2,1,0:T(8,128)S(1)} %get-tuple-element.6), channel_id=1, replica_groups={{1,0,3,2,5,4,7,6},{9,8,11,10,13,12,15,14},{17,16,19,18,21,20,23,22},{25..., dimensions={0} | all-to-all | bytes 524288 | tf_op jit(solution)/shard_map/all_to_all | solution.py:585
  16.1 0.7 %shard_map.87 = f32[8,32,128]{2,1,0:T(8,128)S(1)} custom-call(s32[9]{0:T(128)S(1)} %stack.51.pos_ref, f32[8,2,32,128]{3,2,1,0:T(8,128)S(1)} %all_to_all.15.got_ref.got0), custom_call_target="tpu_custom_call" | custom-call | tf_op jit(solution)/shard_map/pallas_call | solution.py:570
  16.8 10.7 %all_to_all.16.got_ref.got1 = f32[8,32,128]{2,1,0:T(8,128)S(1)} all-to-all(f32[8,32,128]{2,1,0:T(8,128)S(1)} %shard_map.87), channel_id=1, replica_groups={{32,40,48,56,0,8,16,24},{33,41,49,57,1,9,17,25},{34,42,50,58,2,10,18,26..., dimensions={0} | all-to-all | bytes 262144 | tf_op jit(solution)/shard_map/all_to_all | solution.py:585
  27.5 0.0 copy-start.1
  27.5 0.7 %shard_map.88 = f32[8,32,128]{2,1,0:T(8,128)S(1)} custom-call(s32[9]{0:T(128)S(1)} %stack.51.pos_ref, f32[8,32,128]{2,1,0:T(8,128)S(1)} %all_to_all.16.got_ref.got1), custom_call_target="tpu_custom_call" | custom-call | tf_op jit(solution)/shard_map/pallas_call | solution.py:570
  28.2 22.8 %all_to_all.17.got2 = f32[8,32,128]{2,1,0:T(8,128)S(1)} all-to-all(f32[8,32,128]{2,1,0:T(8,128)S(1)} %shard_map.88), channel_id=1, replica_groups={{256,320,384,448,0,64,128,192},{257,321,385,449,1,65,129,193},{258,322,..., dimensions={0} | all-to-all | bytes 262144 | tf_op jit(solution)/shard_map/all_to_all | solution.py:585
  51.0 0.0 copy-done.1
  51.0 3.0 %shard_map.89 = (f32[5,1,512]{2,1,0:T(1,128)}, f32[5,8,512]{2,1,0:T(8,128)}) custom-call(s32[9]{0:T(128)S(1)} %stack.51.pos_ref, f32[8,2,32,128]{3,2,1,0:T(8,128)S(1)} %all_to_all.15.got_ref.got0, f32[8,32,128]{2,1,0:T(8,128)S(1)} %all_to_all.16.got_ref.got1, f32[8,32,128]{2,1,0:T(8,128)S(1)} %all_to_all.17.got2, ...), custom_call_target="tpu_custom_call" | custom-call | tf_op jit(solution)/shard_map/pallas_call | solution.py:570
Async XLA Ops:
  0.6 0.7 %copy-start.5 = (f32[1,5,512]{2,0,1:T(1,128)S(1)}, f32[1,5,512]{2,0,1:T(1,128)}, u32[]{:S(2)}) copy-start(f32[1,5,512]{2,0,1:T(1,128)} %param.7) | copy-start | bytes 30724
  0.6 0.8 %copy-start.3 = (bf16[128,128]{1,0:T(8,128)(2,1)S(1)}, bf16[128,128]{1,0:T(8,128)(2,1)}, u32[]{:S(2)}) copy-start(bf16[128,128]{1,0:T(8,128)(2,1)} %constant.26.clone.place_coarse_ref.spread_ref) | copy-start | bytes 98308
  0.7 0.8 %copy-start.2 = (bf16[128,128]{1,0:T(8,128)(2,1)S(1)}, bf16[128,128]{1,0:T(8,128)(2,1)}, u32[]{:S(2)}) copy-start(bf16[128,128]{1,0:T(8,128)(2,1)} %constant.27.clone.dense_ref.back_coarse_ref) | copy-start | bytes 98308
  0.8 0.7 %copy-start.6 = (s32[1,8]{1,0:T(1,128)S(1)}, s32[1,8]{1,0:T(1,128)}, u32[]{:S(2)}) copy-start(s32[1,8]{1,0:T(1,128)} %param.9) | copy-start | bytes 100
  1.4 0.9 %copy-start = (bf16[256,512]{1,0:T(8,128)(2,1)S(1)}, bf16[256,512]{1,0:T(8,128)(2,1)}, u32[]{:S(2)}) copy-start(bf16[256,512]{1,0:T(8,128)(2,1)} %constant.28.clone.place_ref) | copy-start | bytes 786436
  2.4 0.9 %copy-start.4 = (f32[1,8,5,512]{3,1,2,0:T(8,128)S(1)}, f32[1,8,5,512]{3,1,2,0:T(8,128)}, u32[]{:S(2)}) copy-start(f32[1,8,5,512]{3,1,2,0:T(8,128)} %param.8) | copy-start | bytes 245764
  27.5 23.5 %copy-start.1 = (bf16[512,256]{1,0:T(8,128)(2,1)S(1)}, bf16[512,256]{1,0:T(8,128)(2,1)}, u32[]{:S(2)}) copy-start(bf16[512,256]{1,0:T(8,128)(2,1)} %constant.29.clone.back_ref) | copy-start | bytes 786436

commit v4 on v3

--- a/solution.py
+++ b/solution.py
@@ -27,20 +27,13 @@
 courant = 0.4
 
 
-def placement():
-    fine = np.zeros((256, 512), np.float32)
-    coarse = np.zeros((128, 128), np.float32)
-    for oy in range(2):
-        for oz in range(2):
-            for j in range(8):
-                for k in range(8):
-                    row = oy * 128 + oz * 64 + j * 8 + k
-                    lane = (oy * 4 + j // 2) * PITCH + oz * 4 + k // 2
-                    fine[row, (j % 2 * 2 + k % 2) * 128 + lane] = 1
-    for j in range(8):
-        for k in range(8):
-            coarse[j * 8 + k, j * PITCH + k] = 1
-    return fine, coarse
+def back_matrix():
+    back = np.zeros((512, 256), np.float32)
+    for y in range(16):
+        for z in range(16):
+            row = (y // 8 * 2 + z // 8) * 64 + y % 8 * 8 + z % 8
+            back[(y % 2 * 2 + z % 2) * 128 + y // 2 * PITCH + z // 2, row] = 1
+    return back
 
 
 def place(values, matrix):
@@ -190,9 +183,43 @@
     return jnp.where(flag, second, first), jnp.where(flag, first, second)
 
 
+def whereabouts():
+    device = lax.axis_index("boxes")
+    own = [((device >> (3 * level)) & 7) ^ lead for level, lead in enumerate(LEAD)]
+    first = [(device >> d) & 1 for d in range(3)]
+    second = [(device >> (3 + d)) & 1 for d in range(3)]
+    return own, first, [a == b for a, b in zip(first, second)]
+
+
+def fine_matrix():
+    row = lax.broadcasted_iota(jnp.int32, (256, LANES), 0)
+    lane = lax.broadcasted_iota(jnp.int32, (256, LANES), 1)
+    y = ((row >> 7) << 2) + ((row >> 4) & 3)
+    z = (((row >> 6) & 1) << 2) + ((row >> 1) & 3)
+    hit = lane == y * PITCH + z
+    parity = ((row >> 2) & 2) + (row & 1)
+    return [jnp.where(hit & (parity == q), 1.0, 0.0).astype(jnp.bfloat16) for q in range(4)]
+
+
+def coarse_matrices():
+    row = lax.broadcasted_iota(jnp.int32, (LANES, LANES), 0)
+    lane = lax.broadcasted_iota(jnp.int32, (LANES, LANES), 1)
+    spread = (row < 64) & (lane == (row >> 3) * PITCH + (row & 7))
+    dense = (lane < 64) & (row == (lane >> 3) * PITCH + (lane & 7))
+    return [jnp.where(hit, 1.0, 0.0).astype(jnp.bfloat16) for hit in (spread, dense)]
+
+
+def matrices(place_ref, spread_ref, dense_ref):
+    for q, part in enumerate(fine_matrix()):
+        place_ref[:, q * LANES : (q + 1) * LANES] = part
+    spread_ref[...], dense_ref[...] = coarse_matrices()
+
+
 def prepare(
-    pos_ref, refined_ref, coarse_ref, fine_ref, place_ref, place_coarse_ref, dense_ref, inner_ref, send_ref, scr, scr_c, scr_x
+    refined_ref, coarse_ref, fine_ref, place_ref, spread_ref, dense_ref, inner_ref, send_ref, scr, scr_c, scr_x
 ):
+    places, far, _ = whereabouts()
+    own = places[0]
     lane, x, y, z = positions(8)
     row = lax.broadcasted_iota(jnp.int32, (8, LANES), 0)
     left_half = lane < 64
@@ -217,13 +244,14 @@
         value = scr_c[f]
         rows.append(jnp.where((row & 1) == 1, roll(value, 64, 1), value))
     fine = place(jnp.concatenate(sides[0] + sides[1], axis=0), place_ref[...])
-    coarse = place(jnp.concatenate(rows, axis=0), place_coarse_ref[...])
+    coarse = place(jnp.concatenate(rows, axis=0), spread_ref[...])
     coarse = [coarse[f * 8 : f * 8 + 8] for f in range(5)]
 
     covered = jnp.zeros((8, LANES), jnp.float32)
     for o in range(8):
         here = ((x >= 4) == (o >= 4)) & ((y >= 4) == (o % 4 >= 2)) & ((z >= 4) == (o % 2 == 1))
-        covered = jnp.where(here, (refined_ref[o] > 0).astype(jnp.float32), covered)
+        flag = jnp.broadcast_to(refined_ref[:, o : o + 1], (8, LANES))
+        covered = jnp.where(here & (flag > 0), 1.0, covered)
     state = []
     for f in range(5):
         for q in range(8):
@@ -244,8 +272,6 @@
     for n in range(COUNT):
         inner_ref[n] = stored[n]
 
-    own = pos_ref[0]
-    far = [pos_ref[3 + d] for d in range(3)]
     for t in range(8):
         send_ref[t, 0, FACE - 1 : FACE, :] = fastest[:1]
 
@@ -363,8 +389,8 @@
         send_ref[own ^ pair(d, e), 0:1, :] = value
 
 
-def carry_once(pos_ref, got_ref, send_ref):
-    own, to = pos_ref[0], pos_ref[1]
+def carry_once(got_ref, send_ref):
+    own, to, _ = whereabouts()[0]
     fastest = running_maximum([got_ref[t, 0, FACE - 1 : FACE, :] for t in range(8)])
     faces = [lambda i, j, d=d: got_ref[own ^ (1 << d), 1, i:j, :] for d in range(3)]
 
@@ -375,8 +401,8 @@
     pass_on(send_ref, to, fastest, faces, edges, [edge(d, e, 3) for d, e in PAIRS])
 
 
-def carry_twice(pos_ref, got_ref, send_ref):
-    own, to = pos_ref[1], pos_ref[2]
+def carry_twice(got_ref, send_ref):
+    _, own, to = whereabouts()[0]
     fastest = running_maximum([got_ref[t, FACE - 1 : FACE, :] for t in range(8)])
     faces = [lambda i, j, d=d: got_ref[own ^ (1 << d), i:j, :] for d in range(3)]
 
@@ -390,10 +416,9 @@
     pass_on(send_ref, to, fastest, faces, edges, [far_far(d, e) for d, e in PAIRS])
 
 
-def arrived(pos_ref, got0, got1, got2):
-    own = [pos_ref[i] for i in range(3)]
-    upper_far = [pos_ref[3 + d] == 1 for d in range(3)]
-    twice = [pos_ref[6 + d] == 1 for d in range(3)]
+def arrived(got0, got1, got2):
+    own, first, twice = whereabouts()
+    upper_far = [bit == 1 for bit in first]
     faces = []
     for d in range(3):
         near = got0[own[0] ^ (1 << d), 0]
@@ -421,7 +446,7 @@
     return faces, edges
 
 
-def surround(faces, edges, inner_ref, spread_ref, scr_x):
+def surround(faces, edges, inner_ref, spread, scr_x):
     lane, x, y, z = positions(8)
     row = lax.broadcasted_iota(jnp.int32, (8, LANES), 0)
     left4 = lax.broadcasted_iota(jnp.int32, (32, LANES), 1) < 64
@@ -430,7 +455,7 @@
     for side in range(2):
         value = faces[0][side]
         rows += [jnp.where(left4, value, 0.0), jnp.where(left4, roll(value, 64, 1), 0.0)]
-    scr_x[...] = place(jnp.concatenate(rows, axis=0), spread_ref[...])
+    scr_x[...] = place(jnp.concatenate(rows, axis=0), spread)
     outer = []
     for n in range(COUNT):
         at = n if n < PAIRED else n - PAIRED + 32
@@ -504,15 +529,13 @@
     return [jnp.concatenate([i, o], axis=0) for i, o in zip(inner, outer)]
 
 
-def advance(
-    pos_ref, got0, got1, got2, inner_ref, spread_ref, back_ref, back_coarse_ref, coarse_out, fine_out, scr, scr_x
-):
+def advance(got0, got1, got2, inner_ref, back_ref, spread_ref, dense_ref, coarse_out, fine_out, scr, scr_x):
     lane, x, y, z = positions(16)
     fastest = running_maximum([got2[t, FACE - 1 : FACE, :] for t in range(8)])
     half16 = 0.5 * (courant / jnp.broadcast_to(fastest, (16, LANES)))
     half = half16[:8]
-    faces, edges = arrived(pos_ref, got0, got1, got2)
-    state = surround(faces, edges, inner_ref, spread_ref, scr_x)
+    faces, edges = arrived(got0, got1, got2)
+    state = surround(faces, edges, inner_ref, spread_ref[...], scr_x)
     covered = state[COVER] > 0.5
     fine0 = [[state[f * 8 + q] for f in range(5)] for q in range(8)]
     coarse0 = state[COARSE:DEEP]
@@ -553,7 +576,7 @@
             for ox in range(2):
                 tile = scr[f, pl.ds(ox * 4 + q, 4, stride=8), :]
                 fine_out[f, ox * 4 : ox * 4 + 4, q * 128 : q * 128 + 128] = tile
-    back = place(jnp.concatenate(coarse, axis=0), back_coarse_ref[...])
+    back = place(jnp.concatenate(coarse, axis=0), dense_ref[...])
     for f in range(5):
         value = back[f * 8 : f * 8 + 8]
         value = jnp.where(left_half, value, roll(roll(value, 64, 1), -1, 0))
@@ -565,14 +588,14 @@
     return jax.ShapeDtypeStruct(dims, jnp.float32)
 
 
-def call(kernel, kinds, outs, scratch, args):
-    spaces = {"s": pltpu.SMEM, "v": pltpu.VMEM}
+def call(kernel, outs, scratch, args, cost=None):
     return pl.pallas_call(
         kernel,
         out_shape=outs,
-        in_specs=[pl.BlockSpec(memory_space=spaces[k]) for k in kinds],
+        in_specs=[pl.BlockSpec(memory_space=pltpu.VMEM)] * len(args),
         out_specs=[pl.BlockSpec(memory_space=pltpu.VMEM)] * len(outs),
-        scratch_shapes=[pltpu.VMEM(dims, jnp.float32) for dims in scratch],
+        scratch_shapes=scratch,
+        cost_estimate=cost,
         compiler_params=pltpu.CompilerParams(vmem_limit_bytes=32 * 1024 * 1024),
     )(*args)
 
@@ -586,40 +609,24 @@
 
 
 def local(coarse_state, fine_state, refined):
-    fine_place, coarse_place = placement()
-    as_matrix = lambda m: jnp.asarray(np.ascontiguousarray(m).astype(ml_dtypes.bfloat16))
-    device = lax.axis_index("boxes")
-    levels = [(device >> (3 * level)) & 7 for level in range(3)]
-    bits = [[(level >> d) & 1 for d in range(3)] for level in levels]
-    levels = [level ^ lead for level, lead in zip(levels, LEAD)]
-    twice = [(bits[0][d] == bits[1][d]).astype(jnp.int32) for d in range(3)]
-    pos = jnp.stack(levels + bits[0] + twice).astype(jnp.int32)
-    spread, dense = as_matrix(coarse_place), as_matrix(coarse_place.T)
-
+    back = jnp.asarray(back_matrix().astype(ml_dtypes.bfloat16))
+    fields = lambda *dims: pltpu.VMEM(dims, jnp.float32)
+    matrix = lambda *dims: jax.ShapeDtypeStruct(dims, jnp.bfloat16)
+    made = call(matrices, [matrix(256, 4 * LANES), matrix(LANES, LANES), matrix(LANES, LANES)], [], (), pl.CostEstimate(flops=50000000, bytes_accessed=327680, transcendentals=0))
     inner, send = call(
         prepare,
-        "ssvvvvv",
         [shape(COUNT, 8, LANES), shape(8, 2, ROWS, LANES)],
-        [(5, 32, LANES), (5, 8, LANES), (128, LANES)],
-        (
-            pos,
-            refined[0],
-            jnp.swapaxes(coarse_state, 0, 1),
-            jnp.swapaxes(fine_state[0], 0, 1),
-            as_matrix(fine_place),
-            spread,
-            dense,
-        ),
+        [fields(5, 32, LANES), fields(5, 8, LANES), fields(128, LANES)],
+        (refined, jnp.swapaxes(coarse_state, 0, 1), jnp.swapaxes(fine_state[0], 0, 1), *made),
     )
     got0 = swap(send, 0)
-    got1 = swap(call(carry_once, "sv", [shape(8, ROWS, LANES)], [], (pos, got0))[0], 1)
-    got2 = swap(call(carry_twice, "sv", [shape(8, ROWS, LANES)], [], (pos, got1))[0], 2)
+    got1 = swap(call(carry_once, [shape(8, ROWS, LANES)], [], (got0,))[0], 1)
+    got2 = swap(call(carry_twice, [shape(8, ROWS, LANES)], [], (got1,))[0], 2)
     coarse_out, fine_out = call(
         advance,
-        "svvvvvvv",
         [shape(5, 1, 512), shape(5, 8, 512)],
-        [(5, 32, LANES), (128, LANES)],
-        (pos, got0, got1, got2, inner, spread, as_matrix(fine_place.T), dense),
+        [fields(5, 32, LANES), fields(128, LANES)],
+        (got0, got1, got2, inner, back, *made[1:]),
     )
     return jnp.swapaxes(coarse_out, 0, 1), jnp.swapaxes(fine_out, 0, 1)[None]
 

time: 54.4 us -> 50.4 us (0.926)
  Pallas kernels: 5.73 us -> 3.76 us
  local copies, waits for them, and re-layouts: 2.6 us -> 0.68 us
    pallas_call x4 -> x5, Pallas kernels: 5.73 us -> 3.76 us  [call(): pl.pallas_call(kernel, out_shape=outs, in_specs=[pl.BlockSpec(memory_spac...]
    unnamed x14 -> x8, local copies, waits for them, and re-layouts: 2.51 us -> 0.68 us
where the time goes in v4:
time: 50.4 us; the launch traced here: 50.1 us
  blocking collectives  45 us (89%)
  Pallas kernels  3.76 us (7%)
  between operations  0.69 us (1%)
  local copies, waits for them, and re-layouts  0.68 us (1%)
    all_to_all x3, blocking collectives, swap(): return lax.all_to_all(block, 'boxes', 0, 0, axis_index_groups=groups)  45 us
    pallas_call x5, Pallas kernels, call(): pl.pallas_call(kernel, out_shape=outs, in_specs=[pl.BlockSpec(memory_spac...  3.76 us

profile of v4, /device:TPU:32, one launch (start us, length us, event | category | flops | bytes accessed | tf_op | source)
XLA Modules:
  0.0 50.1 jit_solution(14682324004898984299)
XLA Ops:
  0.6 0.0 copy-start.1
  0.6 0.0 copy-start.2
  0.6 0.2 shard_map.59
  0.8 0.0 copy-start.3
  0.8 0.7 %copy-done.1 = f32[1,8,5,512]{3,1,2,0:T(8,128)S(1)} copy-done((f32[1,8,5,512]{3,1,2,0:T(8,128)S(1)}, f32[1,8,5,512]{3,1,2,0:T(8,128)}, u32[]{:S(2)}) %copy-start.1) | copy-done | bytes 81944
  1.5 0.0 copy-done.2
  1.5 0.0 copy-done.3
  1.5 0.8 %shard_map.60 = (f32[51,8,128]{2,1,0:T(8,128)S(1)}, f32[8,2,32,128]{3,2,1,0:T(8,128)S(1)}) custom-call(s32[1,8]{1,0:T(1,128)S(1)} %copy-done.3, f32[5,1,512]{2,1,0:T(1,128)S(1)} %bitcast.9, f32[5,8,512]{2,1,0:T(8,128)S(1)} %bitcast.8, bf16[256,512]{1,0:T(8,128)(2,1)S(1)} %get-tuple-element.9.place_ref, bf16[128,128]{1,0:T(8,128)(2,1)S(1)} %get-tuple-element.10.spread_ref, ...), custom_call_target="tpu_custom_call" | custom-call | tf_op jit(solution)/shard_map/pallas_call | solution.py:592
  2.3 11.5 %all_to_all.15.got_ref.got0 = f32[8,2,32,128]{3,2,1,0:T(8,128)S(1)} all-to-all(f32[8,2,32,128]{3,2,1,0:T(8,128)S(1)} %get-tuple-element.12), channel_id=1, replica_groups={{1,0,3,2,5,4,7,6},{9,8,11,10,13,12,15,14},{17,16,19,18,21,20,23,22},{25..., dimensions={0} | all-to-all | bytes 524288 | tf_op jit(solution)/shard_map/all_to_all | solution.py:608
  13.8 0.1 shard_map.61
  14.0 10.7 %all_to_all.16.got_ref.got1 = f32[8,32,128]{2,1,0:T(8,128)S(1)} all-to-all(f32[8,32,128]{2,1,0:T(8,128)S(1)} %shard_map.61), channel_id=1, replica_groups={{32,40,48,56,0,8,16,24},{33,41,49,57,1,9,17,25},{34,42,50,58,2,10,18,26..., dimensions={0} | all-to-all | bytes 262144 | tf_op jit(solution)/shard_map/all_to_all | solution.py:608
  24.6 0.0 copy-start
  24.6 0.1 shard_map.62
  24.8 22.8 %all_to_all.17.got2 = f32[8,32,128]{2,1,0:T(8,128)S(1)} all-to-all(f32[8,32,128]{2,1,0:T(8,128)S(1)} %shard_map.62), channel_id=1, replica_groups={{256,320,384,448,0,64,128,192},{257,321,385,449,1,65,129,193},{258,322,..., dimensions={0} | all-to-all | bytes 262144 | tf_op jit(solution)/shard_map/all_to_all | solution.py:608
  47.6 0.0 copy-done
  47.6 2.5 %shard_map.63 = (f32[5,1,512]{2,1,0:T(1,128)}, f32[5,8,512]{2,1,0:T(8,128)}) custom-call(f32[8,2,32,128]{3,2,1,0:T(8,128)S(1)} %all_to_all.15.got_ref.got0, f32[8,32,128]{2,1,0:T(8,128)S(1)} %all_to_all.16.got_ref.got1, f32[8,32,128]{2,1,0:T(8,128)S(1)} %all_to_all.17.got2, f32[51,8,128]{2,1,0:T(8,128)S(1)} %get-tuple-element.13.inner_ref, ...), custom_call_target="tpu_custom_call" | custom-call | tf_op jit(solution)/shard_map/pallas_call | solution.py:592
Async XLA Ops:
  0.6 0.9 %copy-start.1 = (f32[1,8,5,512]{3,1,2,0:T(8,128)S(1)}, f32[1,8,5,512]{3,1,2,0:T(8,128)}, u32[]{:S(2)}) copy-start(f32[1,8,5,512]{3,1,2,0:T(8,128)} %param.5) | copy-start | bytes 245764
  0.6 0.9 %copy-start.2 = (f32[1,5,512]{2,0,1:T(1,128)S(1)}, f32[1,5,512]{2,0,1:T(1,128)}, u32[]{:S(2)}) copy-start(f32[1,5,512]{2,0,1:T(1,128)} %param.4) | copy-start | bytes 30724
  0.8 0.7 %copy-start.3 = (s32[1,8]{1,0:T(1,128)S(1)}, s32[1,8]{1,0:T(1,128)}, u32[]{:S(2)}) copy-start(s32[1,8]{1,0:T(1,128)} %refined_ref.1) | copy-start | bytes 100
  24.6 23.0 %copy-start = (bf16[512,256]{1,0:T(8,128)(2,1)S(1)}, bf16[512,256]{1,0:T(8,128)(2,1)}, u32[]{:S(2)}) copy-start(bf16[512,256]{1,0:T(8,128)(2,1)} %constant.2.clone.back_ref) | copy-start | bytes 786436

commit v5 on v4

--- a/solution.py
+++ b/solution.py
@@ -20,7 +20,7 @@
 ROWS = 32
 MAX_LANE = 120
 PAIRED = 26
-LEAD = (1, 4, 4)
+LEAD = (5, 6, 4)
 SIDES = ((0, 8), (1, -1))
 PAIRS = ((0, 1), (0, 2), (1, 2))
 gamma_gas = 1.4

time: 50.4 us -> 47.5 us (0.942)
  blocking collectives: 45 us -> 42.1 us
    all_to_all x3, blocking collectives: 45 us -> 42.1 us  [swap(): return lax.all_to_all(block, 'boxes', 0, 0, axis_index_groups=groups)]
where the time goes in v5:
time: 47.5 us; the launch traced here: 47.2 us
  blocking collectives  42.1 us (89%)
  Pallas kernels  3.76 us (8%)
  between operations  0.69 us (1%)
  local copies, waits for them, and re-layouts  0.68 us (1%)
    all_to_all x3, blocking collectives, swap(): return lax.all_to_all(block, 'boxes', 0, 0, axis_index_groups=groups)  42.1 us
    pallas_call x5, Pallas kernels, call(): pl.pallas_call(kernel, out_shape=outs, in_specs=[pl.BlockSpec(memory_spac...  3.76 us

profile of v5, /device:TPU:32, one launch (start us, length us, event | category | flops | bytes accessed | tf_op | source)
XLA Modules:
  0.0 47.2 jit_solution(877875356933324659)
XLA Ops:
  0.6 0.0 copy-start.1
  0.6 0.0 copy-start.2
  0.6 0.2 shard_map.59
  0.8 0.0 copy-start.3
  0.8 0.7 %copy-done.1 = f32[1,8,5,512]{3,1,2,0:T(8,128)S(1)} copy-done((f32[1,8,5,512]{3,1,2,0:T(8,128)S(1)}, f32[1,8,5,512]{3,1,2,0:T(8,128)}, u32[]{:S(2)}) %copy-start.1) | copy-done | bytes 81944
  1.5 0.0 copy-done.2
  1.5 0.0 copy-done.3
  1.5 0.8 %shard_map.60 = (f32[51,8,128]{2,1,0:T(8,128)S(1)}, f32[8,2,32,128]{3,2,1,0:T(8,128)S(1)}) custom-call(s32[1,8]{1,0:T(1,128)S(1)} %copy-done.3, f32[5,1,512]{2,1,0:T(1,128)S(1)} %bitcast.9, f32[5,8,512]{2,1,0:T(8,128)S(1)} %bitcast.8, bf16[256,512]{1,0:T(8,128)(2,1)S(1)} %get-tuple-element.9.place_ref, bf16[128,128]{1,0:T(8,128)(2,1)S(1)} %get-tuple-element.10.spread_ref, ...), custom_call_target="tpu_custom_call" | custom-call | tf_op jit(solution)/shard_map/pallas_call | solution.py:592
  2.3 9.6 %all_to_all.15.got_ref.got0 = f32[8,2,32,128]{3,2,1,0:T(8,128)S(1)} all-to-all(f32[8,2,32,128]{3,2,1,0:T(8,128)S(1)} %get-tuple-element.12), channel_id=1, replica_groups={{5,4,7,6,1,0,3,2},{13,12,15,14,9,8,11,10},{21,20,23,22,17,16,19,18},{29..., dimensions={0} | all-to-all | bytes 524288 | tf_op jit(solution)/shard_map/all_to_all | solution.py:608
  11.9 0.1 shard_map.61
  12.0 12.5 %all_to_all.16.got_ref.got1 = f32[8,32,128]{2,1,0:T(8,128)S(1)} all-to-all(f32[8,32,128]{2,1,0:T(8,128)S(1)} %shard_map.61), channel_id=1, replica_groups={{48,56,32,40,16,24,0,8},{49,57,33,41,17,25,1,9},{50,58,34,42,18,26,2,10..., dimensions={0} | all-to-all | bytes 262144 | tf_op jit(solution)/shard_map/all_to_all | solution.py:608
  24.5 0.0 copy-start
  24.5 0.1 shard_map.62
  24.7 20.1 %all_to_all.17.got2 = f32[8,32,128]{2,1,0:T(8,128)S(1)} all-to-all(f32[8,32,128]{2,1,0:T(8,128)S(1)} %shard_map.62), channel_id=1, replica_groups={{256,320,384,448,0,64,128,192},{257,321,385,449,1,65,129,193},{258,322,..., dimensions={0} | all-to-all | bytes 262144 | tf_op jit(solution)/shard_map/all_to_all | solution.py:608
  44.7 0.0 copy-done
  44.7 2.5 %shard_map.63 = (f32[5,1,512]{2,1,0:T(1,128)}, f32[5,8,512]{2,1,0:T(8,128)}) custom-call(f32[8,2,32,128]{3,2,1,0:T(8,128)S(1)} %all_to_all.15.got_ref.got0, f32[8,32,128]{2,1,0:T(8,128)S(1)} %all_to_all.16.got_ref.got1, f32[8,32,128]{2,1,0:T(8,128)S(1)} %all_to_all.17.got2, f32[51,8,128]{2,1,0:T(8,128)S(1)} %get-tuple-element.13.inner_ref, ...), custom_call_target="tpu_custom_call" | custom-call | tf_op jit(solution)/shard_map/pallas_call | solution.py:592
Async XLA Ops:
  0.6 0.9 %copy-start.1 = (f32[1,8,5,512]{3,1,2,0:T(8,128)S(1)}, f32[1,8,5,512]{3,1,2,0:T(8,128)}, u32[]{:S(2)}) copy-start(f32[1,8,5,512]{3,1,2,0:T(8,128)} %param.5) | copy-start | bytes 245764
  0.6 0.9 %copy-start.2 = (f32[1,5,512]{2,0,1:T(1,128)S(1)}, f32[1,5,512]{2,0,1:T(1,128)}, u32[]{:S(2)}) copy-start(f32[1,5,512]{2,0,1:T(1,128)} %param.4) | copy-start | bytes 30724
  0.8 0.7 %copy-start.3 = (s32[1,8]{1,0:T(1,128)S(1)}, s32[1,8]{1,0:T(1,128)}, u32[]{:S(2)}) copy-start(s32[1,8]{1,0:T(1,128)} %refined_ref.1) | copy-start | bytes 100
  24.5 20.2 %copy-start = (bf16[512,256]{1,0:T(8,128)(2,1)S(1)}, bf16[512,256]{1,0:T(8,128)(2,1)}, u32[]{:S(2)}) copy-start(bf16[512,256]{1,0:T(8,128)(2,1)} %constant.2.clone.back_ref) | copy-start | bytes 786436

commit v6 on v5

--- a/solution.py
+++ b/solution.py
@@ -93,28 +93,46 @@
     return roll(x, 1, 0) if d == 0 else roll(x, PITCH if d == 1 else 1, 1)
 
 
-def fine_net(u, inner):
-    prims = [primitive(u[q]) for q in range(8)]
-    total = [None] * 8
-    for d in range(3):
+def fine_net(u, beside, beyond):
+    row = lax.broadcasted_iota(jnp.int32, (8, LANES), 0)
+    prims, prims_beside = [primitive(v) for v in u], [primitive(v) for v in beside]
+    total, total_beside = [None] * 8, [None] * 4
+
+    def add(totals, q, net):
+        totals[q] = net if totals[q] is None else [s + n for s, n in zip(totals[q], net)]
+
+    def minus(left, right):
+        return [a - b for a, b in zip(left, right)]
+
+    def either(flag, first, second):
+        return [jnp.where(flag, a, b) for a, b in zip(first, second)]
+
+    for q in range(4):
+        low, high = cell_flux(u[q], prims[q], 0), cell_flux(u[q + 4], prims[q + 4], 0)
+        near = cell_flux(beside[q], prims_beside[q], 0)
+        middle = face(low, high)
+        after = face(high, either(row == 7, near, [roll(x, -1, 0) for x in low]))
+        first = face(near, low)
+        add(total, q, minus(middle, either(row == 0, first, [roll(x, 1, 0) for x in after])))
+        add(total, q + 4, minus(after, middle))
+        if beyond is not None:
+            next_ = cell_flux(beyond[q], primitive(beyond[q]), 0)
+            outer = face(either(row == 0, next_, near), either(row == 0, near, next_))
+            add(total_beside, q, either(row == 0, minus(first, outer), minus(outer, after)))
+    groups = [(u, prims, total, (0, 4))]
+    if beyond is not None:
+        groups.append((beside, prims_beside, total_beside, (0,)))
+    for d in (1, 2):
         bit = 4 >> d
-        cut = (lambda x: x[:8]) if inner and d > 0 else (lambda x: x)
-        keep = (lambda x: x[:8]) if inner else (lambda x: x)
-        for low in range(8):
-            if low & bit:
-                continue
-            high = low | bit
-            cells = []
-            for q in (low, high):
-                v, pressure, sound = prims[q]
-                cells.append(cell_flux([cut(x) for x in u[q]], ([cut(x) for x in v], cut(pressure), cut(sound)), d))
-            middle = face(cells[0], cells[1])
-            after = face(cells[1], [ahead(x, d) for x in cells[0]])
-            net_low = [keep(middle[f] - behind(after[f], d)) for f in range(5)]
-            net_high = [keep(after[f] - middle[f]) for f in range(5)]
-            for q, net in ((low, net_low), (high, net_high)):
-                total[q] = net if total[q] is None else [s + n for s, n in zip(total[q], net)]
-    return total
+        for cells, prim, totals, starts in groups:
+            for low in [start + q for start in starts for q in range(4) if not q & bit]:
+                high = low | bit
+                left, right = cell_flux(cells[low], prim[low], d), cell_flux(cells[high], prim[high], d)
+                middle = face(left, right)
+                after = face(right, [ahead(x, d) for x in left])
+                add(totals, low, minus(middle, [behind(x, d) for x in after]))
+                add(totals, high, minus(after, middle))
+    return total, total_beside
 
 
 def coarse_net(u, deep, pos):
@@ -135,6 +153,15 @@
         net = [a - b for a, b in zip(after, before)]
         total = net if total is None else [s + n for s, n in zip(total, net)]
     return total
+
+
+def put_faces(send_ref, slot, upper_far, faces):
+    for side, blocks in enumerate(faces):
+        first = pl.multiple_of((upper_far if side == 0 else 1 - upper_far) * 32, 8)
+        for block in range(3):
+            send_ref[slot, pl.ds(first + block * 8, 8), :] = blocks[block]
+    near, far = swapped(upper_far == 1, faces[0][3], faces[1][3])
+    send_ref[slot, 24:32, :] = jnp.concatenate([near[:4], far[:4]], axis=0)
 
 
 def is_deep(n):
@@ -273,7 +300,7 @@
         inner_ref[n] = stored[n]
 
     for t in range(8):
-        send_ref[t, 0, FACE - 1 : FACE, :] = fastest[:1]
+        send_ref[t, FACE - 1 : FACE, :] = fastest[:1]
 
     def taken(n, at, deep_at):
         return (stored[n - 5], deep_at) if is_deep(n) else (stored[n], at)
@@ -286,10 +313,12 @@
     dense = place(scr_x[...], dense_ref[...])
     left4 = lax.broadcasted_iota(jnp.int32, (32, LANES), 1) < 64
     row32 = lax.broadcasted_iota(jnp.int32, (32, LANES), 0)
+    faces_x, faces_y, faces_z = [], [], []
     for side in range(2):
         packed = jnp.where(left4, dense[side * 64 : side * 64 + 32], roll(dense[side * 64 + 32 : side * 64 + 64], 64, 1))
         packed = jnp.where(row32 >= PAIRED, jnp.concatenate([fastest] * 4, axis=0), packed)
-        send_ref[own ^ 1, far[0] if side == 0 else 1 - far[0]] = packed
+        faces_x.append([packed[block * 8 : block * 8 + 8] for block in range(4)])
+    put_faces(send_ref, own ^ 1, far[0], faces_x)
 
     slots = lane - ((lane * 205) >> 11) * PITCH
     corners_xy, corners_xz, corners = [], [], zero
@@ -306,10 +335,7 @@
         width = len(order[3]) * 8
         second = (lane >= width) & (lane < 2 * width)
         blocks[3] = jnp.where(second, roll(roll(blocks[3], width, 1), 4, 0), blocks[3])
-        part = far[1] if side == 0 else 1 - far[1]
-        for block in range(3):
-            send_ref[own ^ 2, part, block * 8 : block * 8 + 8, :] = blocks[block]
-        send_ref[own ^ 2, part, 24:FACE, :] = blocks[3][:4]
+        faces_y.append(blocks)
         corners_xy.append((blocks[0][7:8], jnp.where(lane < 80, blocks[1], blocks[0])[0:1]))
 
         blocks = []
@@ -334,16 +360,15 @@
                 for s, piece in enumerate(pieces):
                     packed = jnp.where((slots == s) & (lane >= 80) & (lane < MAX_LANE), piece, packed)
             blocks.append(packed)
-        part = far[2] if side == 0 else 1 - far[2]
-        for block in range(3):
-            send_ref[own ^ 4, part, block * 8 : block * 8 + 8, :] = blocks[block]
-        send_ref[own ^ 4, part, 24:FACE, :] = blocks[3][:4]
+        faces_z.append(blocks)
         corners_xz.append((blocks[0][7:8], jnp.where(lane < 80, blocks[1], blocks[0])[0:1]))
         for end, first, first_coarse in ((0, 75, 115), (1, 0, 80)):
             to = (side * 2 + end) * 16
             for start, source, i in ((first, blocks[0], 0), (first, blocks[1], 5), (first_coarse, blocks[0], 10)):
                 here = (lane >= to + i) & (lane < to + i + 5)
                 corners = jnp.where(here, roll(source, to + i - start, 1), corners)
+    put_faces(send_ref, own ^ 2, far[1], faces_y)
+    put_faces(send_ref, own ^ 4, far[2], faces_z)
     corners = block_transpose(corners)
 
     edges = [
@@ -356,7 +381,7 @@
         near_near, far_near = swapped(far[d] == 1, upper[0], lower[0])
         near_far, far_far = swapped(far[d] == 1, upper[1], lower[1])
         for r, value in enumerate((near_near, near_far, far_near, far_far)):
-            send_ref[own ^ (1 << d) ^ (1 << e), 0, r : r + 1, :] = value
+            send_ref[own ^ pair(d, e), r : r + 1, :] = value
 
 
 def others(d):
@@ -380,9 +405,8 @@
         send_ref[t, FACE - 1 : FACE, :] = fastest
     for d in range(3):
         slot = own ^ (1 << d)
-        send_ref[slot, : FACE - 1, :] = faces[d](0, FACE - 1)
-        last = faces[d](FACE - 1, FACE)
-        send_ref[slot, FACE - 1 : FACE, :] = jnp.where(lane >= MAX_LANE, fastest, last)
+        send_ref[slot, :FACE, :] = faces[d]
+        send_ref[slot, FACE - 1 : FACE, :] = jnp.where(lane >= MAX_LANE, fastest, faces[d][FACE - 1 : FACE])
         for r, value in enumerate(edges[d]):
             send_ref[slot, FACE + r : FACE + r + 1, :] = value
     for (d, e), value in zip(PAIRS, corners):
@@ -391,11 +415,14 @@
 
 def carry_once(got_ref, send_ref):
     own, to, _ = whereabouts()[0]
-    fastest = running_maximum([got_ref[t, 0, FACE - 1 : FACE, :] for t in range(8)])
-    faces = [lambda i, j, d=d: got_ref[own ^ (1 << d), 1, i:j, :] for d in range(3)]
+    fastest = running_maximum([got_ref[t, FACE - 1 : FACE, :] for t in range(8)])
+    faces = [
+        jnp.concatenate([got_ref[own ^ (1 << d), 32:, :], got_ref[own ^ (1 << d), FACE:32, :]], axis=0)
+        for d in range(3)
+    ]
 
     def edge(d, e, r):
-        return got_ref[own ^ pair(d, e), 0, r : r + 1, :]
+        return got_ref[own ^ pair(d, e), r : r + 1, :]
 
     edges = [[edge(d, e, 1 if e < d else 2) for e in others(d)] for d in range(3)]
     pass_on(send_ref, to, fastest, faces, edges, [edge(d, e, 3) for d, e in PAIRS])
@@ -404,7 +431,7 @@
 def carry_twice(got_ref, send_ref):
     _, own, to = whereabouts()[0]
     fastest = running_maximum([got_ref[t, FACE - 1 : FACE, :] for t in range(8)])
-    faces = [lambda i, j, d=d: got_ref[own ^ (1 << d), i:j, :] for d in range(3)]
+    faces = [got_ref[own ^ (1 << d), :FACE, :] for d in range(3)]
 
     def far_far(d, e):
         return got_ref[own ^ pair(d, e), 0:1, :]
@@ -421,7 +448,7 @@
     upper_far = [bit == 1 for bit in first]
     faces = []
     for d in range(3):
-        near = got0[own[0] ^ (1 << d), 0]
+        near = got0[own[0] ^ (1 << d), :ROWS]
         far = jnp.where(twice[d], got2[own[2] ^ (1 << d)], got1[own[1] ^ (1 << d)])
         faces.append(swapped(upper_far[d], near, far))
 
@@ -434,7 +461,7 @@
     edges = []
     for d, e in PAIRS:
         of_e, of_d = others(d).index(e), others(e).index(d)
-        near_near = got0[own[0] ^ pair(d, e), 0, 0:1, :]
+        near_near = got0[own[0] ^ pair(d, e), 0:1, :]
         near_far = jnp.where(twice[e], again(e, of_d), once(e, of_d))
         far_near = jnp.where(twice[d], again(d, of_e), once(d, of_e))
         both = jnp.where(twice[e], got2[own[2] ^ pair(d, e), 0:1, :], again(d, 2 + of_e))
@@ -456,12 +483,26 @@
         value = faces[0][side]
         rows += [jnp.where(left4, value, 0.0), jnp.where(left4, roll(value, 64, 1), 0.0)]
     scr_x[...] = place(jnp.concatenate(rows, axis=0), spread)
-    outer = []
-    for n in range(COUNT):
-        at = n if n < PAIRED else n - PAIRED + 32
-        above = jnp.broadcast_to(scr_x[at : at + 1, :], (8, LANES))
-        below = jnp.broadcast_to(scr_x[at + 64 : at + 65, :], (8, LANES))
-        outer.append(jnp.where(row == 0, above, below))
+
+    def around(n, above_n=None, upper_row=7):
+        above_n = n if above_n is None else above_n
+        places = [m if m < PAIRED else m - PAIRED + 32 for m in (above_n, n)]
+        above = jnp.broadcast_to(scr_x[places[0] : places[0] + 1, :], (8, LANES))
+        below = jnp.broadcast_to(scr_x[places[1] + 64 : places[1] + 65, :], (8, LANES))
+        return jnp.where(row == upper_row, above, below)
+
+    beside = [[around(f * 8 + 4 + q, f * 8 + q) for f in range(5)] for q in range(4)]
+    beyond = [[around(f * 8 + q, f * 8 + 4 + q) for f in range(5)] for q in range(4)]
+    covered = around(COVER)
+    coarse_outer = [around(n, upper_row=0) for n in range(COARSE, COVER)]
+
+    def put_beside(n, mask, value):
+        f, q = n // 8, n % 4
+        beside[q][f] = jnp.where(mask, value, beside[q][f])
+
+    def put_coarse(f, mask, value):
+        coarse_outer[f] = jnp.where(mask, value, coarse_outer[f])
+
 
     def doubled(value):
         return jnp.concatenate([value[24:28], value[24:28]], axis=0)
@@ -479,11 +520,11 @@
             value = jnp.where(row < 4, roll(last, first - s * 8, 1), roll(last, first - (s + len(order[3])) * 8, 1))
             inner[n] = jnp.where(here, value, inner[n])
         above, below = [jnp.broadcast_to(edges[0][end][side], (8, LANES)) for end in range(2)]
-        edge = jnp.where(row == 0, above, below)
-        for s in range(15):
-            value = roll(edge, first - s * 8, 1)
-            for n in (order[0][s], order[1][s]) if s < 10 else (order[0][s],):
-                outer[n] = jnp.where(here, value, outer[n])
+        edge, coarse_edge = jnp.where(row == 7, above, below), jnp.where(row == 0, above, below)
+        for s in range(10):
+            put_beside(order[0][s], here, roll(edge, first - s * 8, 1))
+        for s in range(10, 15):
+            put_coarse(s - 10, here, roll(coarse_edge, first - s * 8, 1))
 
     columns = jnp.concatenate([edges[2][end][side] for side in range(2) for end in range(2)] * 2, axis=0)
     columns = block_transpose(columns)
@@ -517,16 +558,14 @@
         inner[n] = jnp.where(here, jnp.where(row < 4, upper_rows, lower_rows), inner[n])
 
         above, below = [jnp.broadcast_to(edges[1][end][side], (8, LANES)) for end in range(2)]
-        edge = jnp.where(row == 0, above, below)
+        edge, coarse_edge = jnp.where(row == 7, above, below), joined(jnp.where(row == 0, above, below))
         for s in range(10):
-            value = roll(edge, at - s, 1)
-            for n in (order[0][0][s], order[1][0][s]):
-                outer[n] = jnp.where(here & inside(y), value, outer[n])
-        edge = joined(edge)
+            put_beside(order[0][0][s], here & inside(y), roll(edge, at - s, 1))
         for s in range(5):
-            n = COARSE + s
-            outer[n] = jnp.where(here & inside(y), roll(edge, at - s, 1), outer[n])
-    return [jnp.concatenate([i, o], axis=0) for i, o in zip(inner, outer)]
+            put_coarse(s, here & inside(y), roll(coarse_edge, at - s, 1))
+    fine = [[inner[f * 8 + q] for f in range(5)] for q in range(8)]
+    coarse = [jnp.concatenate([i, o], axis=0) for i, o in zip(inner[COARSE:COVER], coarse_outer)]
+    return fine, beside, beyond, coarse[:5], coarse[5:], inner[COVER] > 0.5, covered > 0.5
 
 
 def advance(got0, got1, got2, inner_ref, back_ref, spread_ref, dense_ref, coarse_out, fine_out, scr, scr_x):
@@ -535,25 +574,29 @@
     half16 = 0.5 * (courant / jnp.broadcast_to(fastest, (16, LANES)))
     half = half16[:8]
     faces, edges = arrived(got0, got1, got2)
-    state = surround(faces, edges, inner_ref, spread_ref[...], scr_x)
-    covered = state[COVER] > 0.5
-    fine0 = [[state[f * 8 + q] for f in range(5)] for q in range(8)]
-    coarse0 = state[COARSE:DEEP]
-
-    net = coarse_net(coarse0, state[DEEP:COVER], (x, y, z))
+    fine0, beside, beyond, coarse0, deep, covered, covered_beside = surround(
+        faces, edges, inner_ref, spread_ref[...], scr_x
+    )
+    row = lax.broadcasted_iota(jnp.int32, (8, LANES), 0)
+
+    net = coarse_net(coarse0, deep, (x, y, z))
     coarse1 = [u - 0.5 * half16 * n for u, n in zip(coarse0, net)]
-    net = fine_net(fine0, False)
-    fine1 = [
-        [jnp.where(covered, fine0[q][f] - half16 * net[q][f], coarse1[f]) for f in range(5)] for q in range(8)
-    ]
+    net, net_beside = fine_net(fine0, beside, beyond)
+
+    def first_section(u, net, covered, coarse):
+        return [jnp.where(covered, a - half * n, c) for a, n, c in zip(u, net, coarse)]
+
+    coarse_beside = [jnp.where(row == 7, roll(c[8:], 7, 0), roll(c[8:], 1, 0)) for c in coarse1]
+    fine1 = [first_section(fine0[q], net[q], covered, [c[:8] for c in coarse1]) for q in range(8)]
+    beside1 = [first_section(beside[q], net_beside[q], covered_beside, coarse_beside) for q in range(4)]
     net = coarse_net(coarse1, None, None)
     coarse2 = [0.5 * c0[:8] + 0.5 * (c1[:8] - 0.5 * half * n[:8]) for c0, c1, n in zip(coarse0, coarse1, net)]
-    net = fine_net(fine1, True)
+    net, _ = fine_net(fine1, beside1, None)
     mine = inside(y[:8]) & inside(z[:8])
-    refined = mine & covered[:8]
+    refined = mine & covered
     fine2 = [
         [
-            jnp.where(refined, 0.5 * fine0[q][f][:8] + 0.5 * (fine1[q][f][:8] - half * net[q][f]), 0.0)
+            jnp.where(refined, 0.5 * fine0[q][f] + 0.5 * (fine1[q][f] - half * net[q][f]), 0.0)
             for f in range(5)
         ]
         for q in range(8)
@@ -615,7 +658,7 @@
     made = call(matrices, [matrix(256, 4 * LANES), matrix(LANES, LANES), matrix(LANES, LANES)], [], (), pl.CostEstimate(flops=50000000, bytes_accessed=327680, transcendentals=0))
     inner, send = call(
         prepare,
-        [shape(COUNT, 8, LANES), shape(8, 2, ROWS, LANES)],
+        [shape(COUNT, 8, LANES), shape(8, 2 * FACE, LANES)],
         [fields(5, 32, LANES), fields(5, 8, LANES), fields(128, LANES)],
         (refined, jnp.swapaxes(coarse_state, 0, 1), jnp.swapaxes(fine_state[0], 0, 1), *made),
     )

time: 47.5 us -> 46.9 us (0.987)
  no operation moved by 1% of the time
where the time goes in v6:
time: 46.9 us; the launch traced here: 46.6 us
  blocking collectives  41.8 us (89%)
  Pallas kernels  3.51 us (7%)
  between operations  0.69 us (1%)
  local copies, waits for them, and re-layouts  0.68 us (1%)
    all_to_all x3, blocking collectives, swap(): return lax.all_to_all(block, 'boxes', 0, 0, axis_index_groups=groups)  41.8 us
    pallas_call x5, Pallas kernels, call(): pl.pallas_call(kernel, out_shape=outs, in_specs=[pl.BlockSpec(memory_spac...  3.51 us

profile of v6, /device:TPU:32, one launch (start us, length us, event | category | flops | bytes accessed | tf_op | source)
XLA Modules:
  0.0 46.6 jit_solution(12527517926053763990)
XLA Ops:
  0.6 0.0 copy-start.1
  0.6 0.0 copy-start.2
  0.6 0.2 shard_map.59
  0.8 0.0 copy-start.3
  0.8 0.7 %copy-done.1 = f32[1,8,5,512]{3,1,2,0:T(8,128)S(1)} copy-done((f32[1,8,5,512]{3,1,2,0:T(8,128)S(1)}, f32[1,8,5,512]{3,1,2,0:T(8,128)}, u32[]{:S(2)}) %copy-start.1) | copy-done | bytes 81944
  1.5 0.0 copy-done.2
  1.5 0.0 copy-done.3
  1.5 0.8 %shard_map.60 = (f32[51,8,128]{2,1,0:T(8,128)S(1)}, f32[8,56,128]{2,1,0:T(8,128)S(1)}) custom-call(s32[1,8]{1,0:T(1,128)S(1)} %copy-done.3, f32[5,1,512]{2,1,0:T(1,128)S(1)} %bitcast.9, f32[5,8,512]{2,1,0:T(8,128)S(1)} %bitcast.8, bf16[256,512]{1,0:T(8,128)(2,1)S(1)} %get-tuple-element.9.place_ref, bf16[128,128]{1,0:T(8,128)(2,1)S(1)} %get-tuple-element.10.spread_ref, ...), custom_call_target="tpu_custom_call" | custom-call | tf_op jit(solution)/shard_map/pallas_call | solution.py:635
  2.3 9.2 %all_to_all.15.got_ref.got0 = f32[8,56,128]{2,1,0:T(8,128)S(1)} all-to-all(f32[8,56,128]{2,1,0:T(8,128)S(1)} %get-tuple-element.12), channel_id=1, replica_groups={{5,4,7,6,1,0,3,2},{13,12,15,14,9,8,11,10},{21,20,23,22,17,16,19,18},{29..., dimensions={0} | all-to-all | bytes 458752 | tf_op jit(solution)/shard_map/all_to_all | solution.py:651
  11.5 0.1 shard_map.61
  11.7 12.5 %all_to_all.16.got_ref.got1 = f32[8,32,128]{2,1,0:T(8,128)S(1)} all-to-all(f32[8,32,128]{2,1,0:T(8,128)S(1)} %shard_map.61), channel_id=1, replica_groups={{48,56,32,40,16,24,0,8},{49,57,33,41,17,25,1,9},{50,58,34,42,18,26,2,10..., dimensions={0} | all-to-all | bytes 262144 | tf_op jit(solution)/shard_map/all_to_all | solution.py:651
  24.2 0.0 copy-start
  24.2 0.1 shard_map.62
  24.3 20.1 %all_to_all.17.got2 = f32[8,32,128]{2,1,0:T(8,128)S(1)} all-to-all(f32[8,32,128]{2,1,0:T(8,128)S(1)} %shard_map.62), channel_id=1, replica_groups={{256,320,384,448,0,64,128,192},{257,321,385,449,1,65,129,193},{258,322,..., dimensions={0} | all-to-all | bytes 262144 | tf_op jit(solution)/shard_map/all_to_all | solution.py:651
  44.4 0.0 copy-done
  44.4 2.3 %shard_map.63 = (f32[5,1,512]{2,1,0:T(1,128)}, f32[5,8,512]{2,1,0:T(8,128)}) custom-call(f32[8,56,128]{2,1,0:T(8,128)S(1)} %all_to_all.15.got_ref.got0, f32[8,32,128]{2,1,0:T(8,128)S(1)} %all_to_all.16.got_ref.got1, f32[8,32,128]{2,1,0:T(8,128)S(1)} %all_to_all.17.got2, f32[51,8,128]{2,1,0:T(8,128)S(1)} %get-tuple-element.13.inner_ref, ...), custom_call_target="tpu_custom_call" | custom-call | tf_op jit(solution)/shard_map/pallas_call | solution.py:635
Async XLA Ops:
  0.6 0.9 %copy-start.1 = (f32[1,8,5,512]{3,1,2,0:T(8,128)S(1)}, f32[1,8,5,512]{3,1,2,0:T(8,128)}, u32[]{:S(2)}) copy-start(f32[1,8,5,512]{3,1,2,0:T(8,128)} %param.5) | copy-start | bytes 245764
  0.6 0.9 %copy-start.2 = (f32[1,5,512]{2,0,1:T(1,128)S(1)}, f32[1,5,512]{2,0,1:T(1,128)}, u32[]{:S(2)}) copy-start(f32[1,5,512]{2,0,1:T(1,128)} %param.4) | copy-start | bytes 30724
  0.8 0.7 %copy-start.3 = (s32[1,8]{1,0:T(1,128)S(1)}, s32[1,8]{1,0:T(1,128)}, u32[]{:S(2)}) copy-start(s32[1,8]{1,0:T(1,128)} %refined_ref.1) | copy-start | bytes 100
  24.2 20.2 %copy-start = (bf16[512,256]{1,0:T(8,128)(2,1)S(1)}, bf16[512,256]{1,0:T(8,128)(2,1)}, u32[]{:S(2)}) copy-start(bf16[512,256]{1,0:T(8,128)(2,1)} %constant.2.clone.back_ref) | copy-start | bytes 786436

commit v7 on v6

--- a/solution.py
+++ b/solution.py
@@ -80,6 +80,15 @@
     return list(u) + flux + [jnp.abs(v[d]) + sound]
 
 
+def moved_cell(u, prim, d, shift):
+    v, pressure, sound = prim
+    u, v_d = [shift(f) for f in u], shift(v[d])
+    pressure = shift(pressure)
+    flux = [u[1 + d]] + [u[1 + e] * v_d for e in range(3)] + [(u[4] + pressure) * v_d]
+    flux[1 + d] = flux[1 + d] + pressure
+    return u + flux + [shift(jnp.abs(v[d]) + sound)]
+
+
 def face(left, right):
     speed = jnp.maximum(left[10], right[10])
     return [(left[5 + f] + right[5 + f]) - speed * (right[f] - left[f]) for f in range(5)]
@@ -111,7 +120,7 @@
         low, high = cell_flux(u[q], prims[q], 0), cell_flux(u[q + 4], prims[q + 4], 0)
         near = cell_flux(beside[q], prims_beside[q], 0)
         middle = face(low, high)
-        after = face(high, either(row == 7, near, [roll(x, -1, 0) for x in low]))
+        after = face(high, either(row == 7, near, moved_cell(u[q], prims[q], 0, lambda x: roll(x, -1, 0))))
         first = face(near, low)
         add(total, q, minus(middle, either(row == 0, first, [roll(x, 1, 0) for x in after])))
         add(total, q + 4, minus(after, middle))
@@ -129,7 +138,7 @@
                 high = low | bit
                 left, right = cell_flux(cells[low], prim[low], d), cell_flux(cells[high], prim[high], d)
                 middle = face(left, right)
-                after = face(right, [ahead(x, d) for x in left])
+                after = face(right, moved_cell(cells[low], prim[low], d, lambda x: ahead(x, d)))
                 add(totals, low, minus(middle, [behind(x, d) for x in after]))
                 add(totals, high, minus(after, middle))
     return total, total_beside
@@ -659,7 +668,7 @@
     inner, send = call(
         prepare,
         [shape(COUNT, 8, LANES), shape(8, 2 * FACE, LANES)],
-        [fields(5, 32, LANES), fields(5, 8, LANES), fields(128, LANES)],
+        [fields(5, 40, LANES), fields(5, 8, LANES), fields(128, LANES)],
         (refined, jnp.swapaxes(coarse_state, 0, 1), jnp.swapaxes(fine_state[0], 0, 1), *made),
     )
     got0 = swap(send, 0)
@@ -668,7 +677,7 @@
     coarse_out, fine_out = call(
         advance,
         [shape(5, 1, 512), shape(5, 8, 512)],
-        [fields(5, 32, LANES), fields(128, LANES)],
+        [fields(5, 40, LANES), fields(128, LANES)],
         (got0, got1, got2, inner, back, *made[1:]),
     )
     return jnp.swapaxes(coarse_out, 0, 1), jnp.swapaxes(fine_out, 0, 1)[None]

time: 46.9 us -> 46.8 us (level)
  no operation moved by 1% of the time
where the time goes in v7:
time: 46.8 us; the launch traced here: 46.6 us
  blocking collectives  41.8 us (89%)
  Pallas kernels  3.45 us (7%)
  between operations  0.69 us (1%)
  local copies, waits for them, and re-layouts  0.68 us (1%)
    all_to_all x3, blocking collectives, swap(): return lax.all_to_all(block, 'boxes', 0, 0, axis_index_groups=groups)  41.8 us
    pallas_call x5, Pallas kernels, call(): pl.pallas_call(kernel, out_shape=outs, in_specs=[pl.BlockSpec(memory_spac...  3.45 us

profile of v7, /device:TPU:32, one launch (start us, length us, event | category | flops | bytes accessed | tf_op | source)
XLA Modules:
  0.0 46.6 jit_solution(7784831799393513760)
XLA Ops:
  0.6 0.0 copy-start.1
  0.6 0.0 copy-start.2
  0.6 0.2 shard_map.59
  0.8 0.0 copy-start.3
  0.8 0.7 %copy-done.1 = f32[1,8,5,512]{3,1,2,0:T(8,128)S(1)} copy-done((f32[1,8,5,512]{3,1,2,0:T(8,128)S(1)}, f32[1,8,5,512]{3,1,2,0:T(8,128)}, u32[]{:S(2)}) %copy-start.1) | copy-done | bytes 81944
  1.5 0.0 copy-done.2
  1.5 0.0 copy-done.3
  1.5 0.8 %shard_map.60 = (f32[51,8,128]{2,1,0:T(8,128)S(1)}, f32[8,56,128]{2,1,0:T(8,128)S(1)}) custom-call(s32[1,8]{1,0:T(1,128)S(1)} %copy-done.3, f32[5,1,512]{2,1,0:T(1,128)S(1)} %bitcast.9, f32[5,8,512]{2,1,0:T(8,128)S(1)} %bitcast.8, bf16[256,512]{1,0:T(8,128)(2,1)S(1)} %get-tuple-element.9.place_ref, bf16[128,128]{1,0:T(8,128)(2,1)S(1)} %get-tuple-element.10.spread_ref, ...), custom_call_target="tpu_custom_call" | custom-call | tf_op jit(solution)/shard_map/pallas_call | solution.py:644
  2.3 9.2 %all_to_all.15.got_ref.got0 = f32[8,56,128]{2,1,0:T(8,128)S(1)} all-to-all(f32[8,56,128]{2,1,0:T(8,128)S(1)} %get-tuple-element.12), channel_id=1, replica_groups={{5,4,7,6,1,0,3,2},{13,12,15,14,9,8,11,10},{21,20,23,22,17,16,19,18},{29..., dimensions={0} | all-to-all | bytes 458752 | tf_op jit(solution)/shard_map/all_to_all | solution.py:660
  11.5 0.1 shard_map.61
  11.7 12.5 %all_to_all.16.got_ref.got1 = f32[8,32,128]{2,1,0:T(8,128)S(1)} all-to-all(f32[8,32,128]{2,1,0:T(8,128)S(1)} %shard_map.61), channel_id=1, replica_groups={{48,56,32,40,16,24,0,8},{49,57,33,41,17,25,1,9},{50,58,34,42,18,26,2,10..., dimensions={0} | all-to-all | bytes 262144 | tf_op jit(solution)/shard_map/all_to_all | solution.py:660
  24.2 0.0 copy-start
  24.2 0.1 shard_map.62
  24.3 20.1 %all_to_all.17.got2 = f32[8,32,128]{2,1,0:T(8,128)S(1)} all-to-all(f32[8,32,128]{2,1,0:T(8,128)S(1)} %shard_map.62), channel_id=1, replica_groups={{256,320,384,448,0,64,128,192},{257,321,385,449,1,65,129,193},{258,322,..., dimensions={0} | all-to-all | bytes 262144 | tf_op jit(solution)/shard_map/all_to_all | solution.py:660
  44.4 0.0 copy-done
  44.4 2.2 %shard_map.63 = (f32[5,1,512]{2,1,0:T(1,128)}, f32[5,8,512]{2,1,0:T(8,128)}) custom-call(f32[8,56,128]{2,1,0:T(8,128)S(1)} %all_to_all.15.got_ref.got0, f32[8,32,128]{2,1,0:T(8,128)S(1)} %all_to_all.16.got_ref.got1, f32[8,32,128]{2,1,0:T(8,128)S(1)} %all_to_all.17.got2, f32[51,8,128]{2,1,0:T(8,128)S(1)} %get-tuple-element.13.inner_ref, ...), custom_call_target="tpu_custom_call" | custom-call | tf_op jit(solution)/shard_map/pallas_call | solution.py:644
Async XLA Ops:
  0.6 0.9 %copy-start.1 = (f32[1,8,5,512]{3,1,2,0:T(8,128)S(1)}, f32[1,8,5,512]{3,1,2,0:T(8,128)}, u32[]{:S(2)}) copy-start(f32[1,8,5,512]{3,1,2,0:T(8,128)} %param.5) | copy-start | bytes 245764
  0.6 0.9 %copy-start.2 = (f32[1,5,512]{2,0,1:T(1,128)S(1)}, f32[1,5,512]{2,0,1:T(1,128)}, u32[]{:S(2)}) copy-start(f32[1,5,512]{2,0,1:T(1,128)} %param.4) | copy-start | bytes 30724
  0.8 0.7 %copy-start.3 = (s32[1,8]{1,0:T(1,128)S(1)}, s32[1,8]{1,0:T(1,128)}, u32[]{:S(2)}) copy-start(s32[1,8]{1,0:T(1,128)} %refined_ref.1) | copy-start | bytes 100
  24.2 20.2 %copy-start = (bf16[512,256]{1,0:T(8,128)(2,1)S(1)}, bf16[512,256]{1,0:T(8,128)(2,1)}, u32[]{:S(2)}) copy-start(bf16[512,256]{1,0:T(8,128)(2,1)} %constant.2.clone.back_ref) | copy-start | bytes 786436

commit v8 on v7

--- a/solution.py
+++ b/solution.py
@@ -144,11 +144,14 @@
     return total, total_beside
 
 
-def coarse_net(u, deep, pos):
+def coarse_net(u, deep, pos, inner=False):
     prim = primitive(u)
     prim_deep = None if deep is None else primitive(deep)
     total = None
     for d in range(3):
+        if inner and d == 1:
+            u, prim = [x[:8] for x in u], ([x[:8] for x in prim[0]], prim[1][:8], prim[2][:8])
+            total = [x[:8] for x in total]
         cell = cell_flux(u, prim, d)
         right = [ahead(x, d) for x in cell]
         if deep is not None:
@@ -598,7 +601,7 @@
     coarse_beside = [jnp.where(row == 7, roll(c[8:], 7, 0), roll(c[8:], 1, 0)) for c in coarse1]
     fine1 = [first_section(fine0[q], net[q], covered, [c[:8] for c in coarse1]) for q in range(8)]
     beside1 = [first_section(beside[q], net_beside[q], covered_beside, coarse_beside) for q in range(4)]
-    net = coarse_net(coarse1, None, None)
+    net = coarse_net(coarse1, None, None, True)
     coarse2 = [0.5 * c0[:8] + 0.5 * (c1[:8] - 0.5 * half * n[:8]) for c0, c1, n in zip(coarse0, coarse1, net)]
     net, _ = fine_net(fine1, beside1, None)
     mine = inside(y[:8]) & inside(z[:8])

time: 46.8 us -> 46.8 us (level)
  no operation moved by 1% of the time
where the time goes in v8:
time: 46.8 us; the launch traced here: 46.6 us
  blocking collectives  41.8 us (89%)
  Pallas kernels  3.45 us (7%)
  between operations  0.69 us (1%)
  local copies, waits for them, and re-layouts  0.68 us (1%)
    all_to_all x3, blocking collectives, swap(): return lax.all_to_all(block, 'boxes', 0, 0, axis_index_groups=groups)  41.8 us
    pallas_call x5, Pallas kernels, call(): pl.pallas_call(kernel, out_shape=outs, in_specs=[pl.BlockSpec(memory_spac...  3.45 us

profile of v8, /device:TPU:32, one launch (start us, length us, event | category | flops | bytes accessed | tf_op | source)
XLA Modules:
  0.0 46.6 jit_solution(7784831799393513760)
XLA Ops:
  0.6 0.0 copy-start.1
  0.6 0.0 copy-start.2
  0.6 0.2 shard_map.59
  0.8 0.0 copy-start.3
  0.8 0.7 %copy-done.1 = f32[1,8,5,512]{3,1,2,0:T(8,128)S(1)} copy-done((f32[1,8,5,512]{3,1,2,0:T(8,128)S(1)}, f32[1,8,5,512]{3,1,2,0:T(8,128)}, u32[]{:S(2)}) %copy-start.1) | copy-done | bytes 81944
  1.5 0.0 copy-done.2
  1.5 0.0 copy-done.3
  1.5 0.8 %shard_map.60 = (f32[51,8,128]{2,1,0:T(8,128)S(1)}, f32[8,56,128]{2,1,0:T(8,128)S(1)}) custom-call(s32[1,8]{1,0:T(1,128)S(1)} %copy-done.3, f32[5,1,512]{2,1,0:T(1,128)S(1)} %bitcast.9, f32[5,8,512]{2,1,0:T(8,128)S(1)} %bitcast.8, bf16[256,512]{1,0:T(8,128)(2,1)S(1)} %get-tuple-element.9.place_ref, bf16[128,128]{1,0:T(8,128)(2,1)S(1)} %get-tuple-element.10.spread_ref, ...), custom_call_target="tpu_custom_call" | custom-call | tf_op jit(solution)/shard_map/pallas_call | solution.py:647
  2.3 9.2 %all_to_all.15.got_ref.got0 = f32[8,56,128]{2,1,0:T(8,128)S(1)} all-to-all(f32[8,56,128]{2,1,0:T(8,128)S(1)} %get-tuple-element.12), channel_id=1, replica_groups={{5,4,7,6,1,0,3,2},{13,12,15,14,9,8,11,10},{21,20,23,22,17,16,19,18},{29..., dimensions={0} | all-to-all | bytes 458752 | tf_op jit(solution)/shard_map/all_to_all | solution.py:663
  11.5 0.1 shard_map.61
  11.7 12.5 %all_to_all.16.got_ref.got1 = f32[8,32,128]{2,1,0:T(8,128)S(1)} all-to-all(f32[8,32,128]{2,1,0:T(8,128)S(1)} %shard_map.61), channel_id=1, replica_groups={{48,56,32,40,16,24,0,8},{49,57,33,41,17,25,1,9},{50,58,34,42,18,26,2,10..., dimensions={0} | all-to-all | bytes 262144 | tf_op jit(solution)/shard_map/all_to_all | solution.py:663
  24.2 0.0 copy-start
  24.2 0.1 shard_map.62
  24.3 20.1 %all_to_all.17.got2 = f32[8,32,128]{2,1,0:T(8,128)S(1)} all-to-all(f32[8,32,128]{2,1,0:T(8,128)S(1)} %shard_map.62), channel_id=1, replica_groups={{256,320,384,448,0,64,128,192},{257,321,385,449,1,65,129,193},{258,322,..., dimensions={0} | all-to-all | bytes 262144 | tf_op jit(solution)/shard_map/all_to_all | solution.py:663
  44.4 0.0 copy-done
  44.4 2.2 %shard_map.63 = (f32[5,1,512]{2,1,0:T(1,128)}, f32[5,8,512]{2,1,0:T(8,128)}) custom-call(f32[8,56,128]{2,1,0:T(8,128)S(1)} %all_to_all.15.got_ref.got0, f32[8,32,128]{2,1,0:T(8,128)S(1)} %all_to_all.16.got_ref.got1, f32[8,32,128]{2,1,0:T(8,128)S(1)} %all_to_all.17.got2, f32[51,8,128]{2,1,0:T(8,128)S(1)} %get-tuple-element.13.inner_ref, ...), custom_call_target="tpu_custom_call" | custom-call | tf_op jit(solution)/shard_map/pallas_call | solution.py:647
Async XLA Ops:
  0.6 0.9 %copy-start.1 = (f32[1,8,5,512]{3,1,2,0:T(8,128)S(1)}, f32[1,8,5,512]{3,1,2,0:T(8,128)}, u32[]{:S(2)}) copy-start(f32[1,8,5,512]{3,1,2,0:T(8,128)} %param.5) | copy-start | bytes 245764
  0.6 0.9 %copy-start.2 = (f32[1,5,512]{2,0,1:T(1,128)S(1)}, f32[1,5,512]{2,0,1:T(1,128)}, u32[]{:S(2)}) copy-start(f32[1,5,512]{2,0,1:T(1,128)} %param.4) | copy-start | bytes 30724
  0.8 0.7 %copy-start.3 = (s32[1,8]{1,0:T(1,128)S(1)}, s32[1,8]{1,0:T(1,128)}, u32[]{:S(2)}) copy-start(s32[1,8]{1,0:T(1,128)} %refined_ref.1) | copy-start | bytes 100
  24.2 20.2 %copy-start = (bf16[512,256]{1,0:T(8,128)(2,1)S(1)}, bf16[512,256]{1,0:T(8,128)(2,1)}, u32[]{:S(2)}) copy-start(bf16[512,256]{1,0:T(8,128)(2,1)} %constant.2.clone.back_ref) | copy-start | bytes 786436

commit v9 on v8

--- a/solution.py
+++ b/solution.py
@@ -404,8 +404,12 @@
     return (1 << d) ^ (1 << e)
 
 
+def so_far(rows):
+    return functools.reduce(jnp.maximum, rows)
+
+
 def running_maximum(rows):
-    fastest = functools.reduce(jnp.maximum, rows)
+    fastest = so_far(rows)
     lane = lax.broadcasted_iota(jnp.int32, fastest.shape, 1)
     fastest = jnp.where(lane >= MAX_LANE, fastest, 0.0)
     return jnp.broadcast_to(jnp.max(fastest), (1, LANES))
@@ -427,7 +431,7 @@
 
 def carry_once(got_ref, send_ref):
     own, to, _ = whereabouts()[0]
-    fastest = running_maximum([got_ref[t, FACE - 1 : FACE, :] for t in range(8)])
+    fastest = so_far([got_ref[t, FACE - 1 : FACE, :] for t in range(8)])
     faces = [
         jnp.concatenate([got_ref[own ^ (1 << d), 32:, :], got_ref[own ^ (1 << d), FACE:32, :]], axis=0)
         for d in range(3)
@@ -442,7 +446,7 @@
 
 def carry_twice(got_ref, send_ref):
     _, own, to = whereabouts()[0]
-    fastest = running_maximum([got_ref[t, FACE - 1 : FACE, :] for t in range(8)])
+    fastest = so_far([got_ref[t, FACE - 1 : FACE, :] for t in range(8)])
     faces = [got_ref[own ^ (1 << d), :FACE, :] for d in range(3)]
 
     def far_far(d, e):

time: 46.8 us -> 46.7 us (level)
  no operation moved by 1% of the time
where the time goes in v9:
time: 46.7 us; the launch traced here: 46.5 us
  blocking collectives  41.9 us (90%)
  Pallas kernels  3.22 us (7%)
  local copies, waits for them, and re-layouts  0.68 us (1%)
  between operations  0.68 us (1%)
    all_to_all x3, blocking collectives, swap(): return lax.all_to_all(block, 'boxes', 0, 0, axis_index_groups=groups)  41.9 us
    pallas_call x5, Pallas kernels, call(): pl.pallas_call(kernel, out_shape=outs, in_specs=[pl.BlockSpec(memory_spac...  3.22 us

profile of v9, /device:TPU:32, one launch (start us, length us, event | category | flops | bytes accessed | tf_op | source)
XLA Modules:
  0.0 46.5 jit_solution(17993833296383131539)
XLA Ops:
  0.6 0.0 copy-start.1
  0.6 0.0 copy-start.2
  0.6 0.2 shard_map.59
  0.8 0.0 copy-start.3
  0.8 0.7 %copy-done.1 = f32[1,8,5,512]{3,1,2,0:T(8,128)S(1)} copy-done((f32[1,8,5,512]{3,1,2,0:T(8,128)S(1)}, f32[1,8,5,512]{3,1,2,0:T(8,128)}, u32[]{:S(2)}) %copy-start.1) | copy-done | bytes 81944
  1.5 0.0 copy-done.2
  1.5 0.0 copy-done.3
  1.5 0.8 %shard_map.60 = (f32[51,8,128]{2,1,0:T(8,128)S(1)}, f32[8,56,128]{2,1,0:T(8,128)S(1)}) custom-call(s32[1,8]{1,0:T(1,128)S(1)} %copy-done.3, f32[5,1,512]{2,1,0:T(1,128)S(1)} %bitcast.9, f32[5,8,512]{2,1,0:T(8,128)S(1)} %bitcast.8, bf16[256,512]{1,0:T(8,128)(2,1)S(1)} %get-tuple-element.9.place_ref, bf16[128,128]{1,0:T(8,128)(2,1)S(1)} %get-tuple-element.10.spread_ref, ...), custom_call_target="tpu_custom_call" | custom-call | tf_op jit(solution)/shard_map/pallas_call | solution.py:651
  2.3 9.2 %all_to_all.15.got_ref.got0 = f32[8,56,128]{2,1,0:T(8,128)S(1)} all-to-all(f32[8,56,128]{2,1,0:T(8,128)S(1)} %get-tuple-element.12), channel_id=1, replica_groups={{5,4,7,6,1,0,3,2},{13,12,15,14,9,8,11,10},{21,20,23,22,17,16,19,18},{29..., dimensions={0} | all-to-all | bytes 458752 | tf_op jit(solution)/shard_map/all_to_all | solution.py:667
  11.6 12.5 %all_to_all.16.got_ref.got1 = f32[8,32,128]{2,1,0:T(8,128)S(1)} all-to-all(f32[8,32,128]{2,1,0:T(8,128)S(1)} %shard_map.61), channel_id=1, replica_groups={{48,56,32,40,16,24,0,8},{49,57,33,41,17,25,1,9},{50,58,34,42,18,26,2,10..., dimensions={0} | all-to-all | bytes 262144 | tf_op jit(solution)/shard_map/all_to_all | solution.py:667
  24.1 0.0 copy-start
  24.1 20.2 %all_to_all.17.got2 = f32[8,32,128]{2,1,0:T(8,128)S(1)} all-to-all(f32[8,32,128]{2,1,0:T(8,128)S(1)} %shard_map.62), channel_id=1, replica_groups={{256,320,384,448,0,64,128,192},{257,321,385,449,1,65,129,193},{258,322,..., dimensions={0} | all-to-all | bytes 262144 | tf_op jit(solution)/shard_map/all_to_all | solution.py:667
  44.3 0.0 copy-done
  44.3 2.2 %shard_map.63 = (f32[5,1,512]{2,1,0:T(1,128)}, f32[5,8,512]{2,1,0:T(8,128)}) custom-call(f32[8,56,128]{2,1,0:T(8,128)S(1)} %all_to_all.15.got_ref.got0, f32[8,32,128]{2,1,0:T(8,128)S(1)} %all_to_all.16.got_ref.got1, f32[8,32,128]{2,1,0:T(8,128)S(1)} %all_to_all.17.got2, f32[51,8,128]{2,1,0:T(8,128)S(1)} %get-tuple-element.13.inner_ref, ...), custom_call_target="tpu_custom_call" | custom-call | tf_op jit(solution)/shard_map/pallas_call | solution.py:651
  (2 shorter events, 0.0 us)
Async XLA Ops:
  0.6 0.9 %copy-start.1 = (f32[1,8,5,512]{3,1,2,0:T(8,128)S(1)}, f32[1,8,5,512]{3,1,2,0:T(8,128)}, u32[]{:S(2)}) copy-start(f32[1,8,5,512]{3,1,2,0:T(8,128)} %param.5) | copy-start | bytes 245764
  0.6 0.9 %copy-start.2 = (f32[1,5,512]{2,0,1:T(1,128)S(1)}, f32[1,5,512]{2,0,1:T(1,128)}, u32[]{:S(2)}) copy-start(f32[1,5,512]{2,0,1:T(1,128)} %param.4) | copy-start | bytes 30724
  0.8 0.7 %copy-start.3 = (s32[1,8]{1,0:T(1,128)S(1)}, s32[1,8]{1,0:T(1,128)}, u32[]{:S(2)}) copy-start(s32[1,8]{1,0:T(1,128)} %refined_ref.1) | copy-start | bytes 100
  24.1 20.2 %copy-start = (bf16[512,256]{1,0:T(8,128)(2,1)S(1)}, bf16[512,256]{1,0:T(8,128)(2,1)}, u32[]{:S(2)}) copy-start(bf16[512,256]{1,0:T(8,128)(2,1)} %constant.2.clone.back_ref) | copy-start | bytes 786436
